TPU v7x, 32 devices: a whole 2x2x4 slice. The times are simulated.
32 devices in a mesh: band: 4 (over z), trial: 8 (over y, x, core).
Axes of the slice: x: 2, y: 2, z: 4, core: 2. Of those that a mesh axis runs over, the one named last changes fastest.
Arguments:
- intensity: bfloat16 [2, 16384, 2048], P(None, 'band', 'trial'), may hold values from -6 to 6
- fine_delay: int32 [32, 32, 512], P('band'), may hold values from 0 to 31
- span_start: int32 [8, 32], replicated, may hold values from 0 to 28
- sub_rel: int32 [512, 32], P('trial'), may hold values from 0 to 3
- offset: int32 [512, 32], P('trial'), may hold values from 0 to 1024
- widths: int32 [4], replicated, may hold values from 1 to 64
Outputs:
- series: bfloat16 [2, 512, 2048], P(None, ('trial', 'band'))
- peaks: float32 [2, 512, 4], P(None, ('trial', 'band'))
All inputs are finite; a program needn't handle non-finite values.
Results may differ from a plain program's by a relative error of at most 0.014.
Values may be sent and summed in bfloat16 or wider, within the bound.
No kernel may reach another device: no remote copies, remote signals or barrier semaphores. Data moves between devices by JAX's collectives and lax.ppermute only.
A program may use at most 64 MiB of HBM per device.

v0:
```python
import functools
import math

import jax
import jax.numpy as jnp
from jax import lax
from jax.experimental import pallas as pl
from jax.experimental.pallas import tpu as pltpu
from jax.sharding import PartitionSpec as P

QSPAN = 4
MAXD1 = 32
LANES = 128


def round_up(number, step):
    return (number + step - 1) // step * step


def fine_kernel(subs, trials_axis, rows, span_ref, x_ref, delay_ref, out_ref, lagged_ref, part_ref, send_ref):
    sub = pl.program_id(0)
    beams, width, block_len = x_ref.shape
    q_count = delay_ref.shape[1]
    halves = block_len // LANES
    lane = lax.broadcasted_iota(jnp.int32, (8, LANES), 1)
    delays = delay_ref[0]
    selector = jnp.concatenate(
        [(delays == lag).astype(jnp.bfloat16) for lag in range(MAXD1)], axis=0
    )
    for beam in range(beams):
        lagged_ref[...] = jnp.dot(selector, x_ref[beam], preferred_element_type=jnp.float32)
        for group in range(q_count // 8):
            sums = [jnp.zeros((8, LANES), jnp.float32) for _ in range(halves + 1)]
            for lag in range(MAXD1):
                base = lag * q_count + group * 8
                for half in range(halves):
                    piece = lagged_ref[base : base + 8, half * LANES : (half + 1) * LANES]
                    if lag == 0:
                        sums[half + 1] = sums[half + 1] + piece
                        continue
                    moved = pltpu.roll(piece, LANES - lag, 1)
                    stays = lane < LANES - lag
                    sums[half + 1] = sums[half + 1] + jnp.where(stays, moved, 0.0)
                    sums[half] = sums[half] + jnp.where(stays, 0.0, moved)
            before = sums[0]
            before = before + pltpu.roll(before, 32, 1)
            sums[0] = before + pltpu.roll(before, 64, 1)
            for piece in range(halves + 1):
                part_ref[beam, piece, group * 8 : group * 8 + 8, :] = sums[piece]
    own = lax.axis_index("band") * subs + sub
    row_id = lax.broadcasted_iota(jnp.int32, (QSPAN, LANES), 0)
    lane_part = lax.broadcasted_iota(jnp.int32, (QSPAN, LANES), 1) // MAXD1
    main = subs * beams * halves * QSPAN
    for target in range(trials_axis):
        start = span_ref[target, own]
        for beam in range(beams):
            for half in range(halves):
                place = (sub * beams + beam) * halves * QSPAN + half * QSPAN
                send_ref[pl.ds(target * rows + place, QSPAN), :] = part_ref[
                    beam, half + 1, pl.ds(start, QSPAN), :
                ]
            tails = part_ref[beam, 0, pl.ds(start, QSPAN), :]
            tails = jnp.sum(jnp.where(row_id == lane_part, tails, 0.0), axis=0, keepdims=True)
            send_ref[pl.ds(target * rows + main + sub * beams + beam, 1), :] = tails

    @pl.when(sub == subs - 1)
    def _():
        for target in range(trials_axis):
            out_ref[target] = send_ref[target * rows : (target + 1) * rows].astype(jnp.bfloat16)


def trial_kernel(subs, beams, bands, rel_ref, offset_ref, recv_ref, out_ref, flat_ref, wide_ref, sums_ref):
    sources, rows, _ = recv_ref.shape
    trials = rel_ref.shape[0]
    halves = 2
    blocks = sources * halves
    stride = wide_ref.shape[1]
    main = subs * beams * halves * QSPAN
    lane = lax.broadcasted_iota(jnp.int32, (8, LANES), 1)
    for source in range(sources):
        flat_ref[source * rows : (source + 1) * rows] = recv_ref[source].astype(jnp.float32)
    flat_ref[sources * rows :] = jnp.zeros((rows, LANES), jnp.float32)
    lane_all = lax.broadcasted_iota(jnp.int32, (sources, LANES), 1)
    for sub in range(subs):
        for beam in range(beams):
            pair = sub * beams + beam
            tails = flat_ref[pl.ds(rows + main + pair, sources, stride=rows), :]
            for span in range(QSPAN):
                row = pair * QSPAN + span
                wide_ref[row, blocks:, :] = jnp.zeros((stride - blocks, LANES), jnp.float32)
                for half in range(halves):
                    piece = flat_ref[
                        pl.ds(pair * halves * QSPAN + half * QSPAN + span, sources, stride=rows), :
                    ]
                    if half == halves - 1:
                        turn = (LANES - MAXD1 - span * MAXD1) % LANES
                        moved = pltpu.roll(tails, turn, 1) if turn else tails
                        piece = piece + jnp.where(lane_all >= LANES - MAXD1, moved, 0.0)
                    wide_ref[row, pl.ds(half, sources, stride=halves), :] = piece
    first = lax.axis_index("band") * subs
    per_band = trials // bands
    step_rows = beams * per_band

    def one_trial(trial, carry):
        sums = [[jnp.zeros((8, LANES), jnp.float32) for _ in range(blocks // 8)] for _ in range(beams)]
        for sub in range(subs):
            span = rel_ref[trial, first + sub]
            shift = offset_ref[trial, first + sub]
            coarse = shift // LANES
            fine = shift - coarse * LANES
            keep = lane >= fine
            turn = (LANES - fine) % LANES
            for beam in range(beams):
                row = (sub * beams + beam) * QSPAN + span
                for part in range(blocks // 8):
                    near = wide_ref[row, pl.ds(coarse + part * 8, 8), :]
                    far = wide_ref[row, pl.ds(coarse + part * 8 + 1, 8), :]
                    moved = pltpu.roll(jnp.where(keep, near, far), turn, 1)
                    sums[beam][part] = sums[beam][part] + moved
        band = trial // per_band
        inside = trial - band * per_band
        for beam in range(beams):
            for part in range(blocks // 8):
                start = (band * blocks + part * 8) * step_rows + beam * per_band + inside
                sums_ref[pl.ds(start, 8, stride=step_rows), :] = sums[beam][part]
        return carry

    lax.fori_loop(0, trials, one_trial, 0)
    out_ref[...] = sums_ref[...].astype(jnp.bfloat16)


def peak_kernel(beams, scale, width_ref, x_ref, series_ref, peak_ref):
    blocks, rows, _ = x_ref.shape
    per_beam = rows // beams
    series = [(x_ref[block].astype(jnp.float32) / scale).astype(jnp.bfloat16) for block in range(blocks)]
    for block in range(blocks):
        for beam in range(beams):
            series_ref[beam, :, block * LANES : (block + 1) * LANES] = (
                series[block].astype(jnp.float32)[beam * per_beam : (beam + 1) * per_beam].astype(jnp.bfloat16)
            )
    following = series[1:] + [jnp.zeros_like(series[0])]
    left = jnp.concatenate(
        [jnp.concatenate([here, after], axis=1) for here, after in zip(series, following)], axis=0
    )
    source = lax.broadcasted_iota(jnp.int32, (2 * LANES, LANES), 0)
    place = lax.broadcasted_iota(jnp.int32, (2 * LANES, LANES), 1)
    slot_id = lax.broadcasted_iota(jnp.int32, (rows, peak_ref.shape[2]), 1)
    peaks = jnp.zeros((rows, peak_ref.shape[2]), jnp.float32)
    for slot in range(peak_ref.shape[2]):
        width = width_ref[slot]
        window = ((source >= place) & (source < place + width)).astype(jnp.bfloat16)
        totals = jnp.dot(left, window, preferred_element_type=jnp.float32)
        best = totals[:rows]
        for block in range(1, blocks):
            best = jnp.maximum(best, totals[block * rows : (block + 1) * rows])
        best = jnp.max(best, axis=1, keepdims=True)
        root = jnp.sqrt(jnp.full((rows, 1), width, jnp.int32).astype(jnp.float32))
        peaks = jnp.where(slot_id == slot, best / root, peaks)
    for beam in range(beams):
        peak_ref[beam] = peaks[beam * per_beam : (beam + 1) * per_beam]


def local(intensity, fine_delay, span_start, sub_rel, offset, widths):
    beams, channels, block_len = intensity.shape
    subs, q_count, width = fine_delay.shape
    sources = lax.axis_size("trial")
    bands = lax.axis_size("band")
    trials = sub_rel.shape[0]
    halves = block_len // LANES
    blocks = sources * halves
    length = sources * block_len
    main = subs * beams * halves * QSPAN
    rows = round_up(main + subs * beams, 16)
    send = pl.pallas_call(
        functools.partial(fine_kernel, subs, sources, rows),
        grid_spec=pltpu.PrefetchScalarGridSpec(
            num_scalar_prefetch=1,
            grid=(subs,),
            in_specs=[
                pl.BlockSpec((beams, width, block_len), lambda sub, span: (0, sub, 0)),
                pl.BlockSpec((1, q_count, width), lambda sub, span: (sub, 0, 0)),
            ],
            out_specs=pl.BlockSpec((sources, rows, LANES), lambda sub, span: (0, 0, 0)),
            scratch_shapes=[
                pltpu.VMEM((MAXD1 * q_count, block_len), jnp.float32),
                pltpu.VMEM((beams, halves + 1, q_count, LANES), jnp.float32),
                pltpu.VMEM((sources * rows, LANES), jnp.float32),
            ],
        ),
        out_shape=jax.ShapeDtypeStruct((sources, rows, LANES), jnp.bfloat16),
        compiler_params=pltpu.CompilerParams(vmem_limit_bytes=48 << 20),
        name="fine_delays",
    )(span_start, intensity, fine_delay)
    received = lax.all_to_all(send, "trial", split_axis=0, concat_axis=0, tiled=True)
    stride = round_up(blocks + length // 2 // LANES + 1, 8)
    per_band = trials // bands
    sums = pl.pallas_call(
        functools.partial(trial_kernel, subs, beams, bands),
        in_specs=[
            pl.BlockSpec(memory_space=pltpu.SMEM),
            pl.BlockSpec(memory_space=pltpu.SMEM),
            pl.BlockSpec(memory_space=pltpu.VMEM),
        ],
        out_specs=pl.BlockSpec(memory_space=pltpu.VMEM),
        scratch_shapes=[
            pltpu.VMEM(((sources + 1) * rows, LANES), jnp.float32),
            pltpu.VMEM((subs * beams * QSPAN, stride, LANES), jnp.float32),
            pltpu.VMEM((blocks * beams * trials, LANES), jnp.float32),
        ],
        out_shape=jax.ShapeDtypeStruct((blocks * beams * trials, LANES), jnp.bfloat16),
        compiler_params=pltpu.CompilerParams(vmem_limit_bytes=48 << 20),
        name="trial_sums",
    )(sub_rel, offset, received)
    summed = lax.psum_scatter(sums, "band", scatter_dimension=0, tiled=True)
    summed = summed.reshape(blocks, beams * per_band, LANES)
    return pl.pallas_call(
        functools.partial(peak_kernel, beams, math.sqrt(channels * bands)),
        in_specs=[
            pl.BlockSpec(memory_space=pltpu.SMEM),
            pl.BlockSpec(memory_space=pltpu.VMEM),
        ],
        out_specs=[pl.BlockSpec(memory_space=pltpu.VMEM)] * 2,
        out_shape=[
            jax.ShapeDtypeStruct((beams, per_band, length), jnp.bfloat16),
            jax.ShapeDtypeStruct((beams, per_band, widths.shape[0]), jnp.float32),
        ],
        compiler_params=pltpu.CompilerParams(vmem_limit_bytes=48 << 20),
        name="boxcar_peaks",
    )(widths, summed)


def solution(mesh):
    return jax.shard_map(
        lambda *arrays: tuple(local(*arrays)),
        mesh=mesh,
        in_specs=(
            P(None, "band", "trial"),
            P("band", None, None),
            P(),
            P("trial", None),
            P("trial", None),
            P(),
        ),
        out_specs=(P(None, ("trial", "band"), None), P(None, ("trial", "band"), None)),
        check_vma=False,
    )
```

profile of v0, /device:TPU:0, one launch (start us, length us, event | category | flops | bytes accessed | tf_op | source)
XLA Modules:
  0.0 78.6 jit_solution(17803128272245683342)
XLA Ops:
  7.2 0.0 copy-start
  7.2 2.2 %copy-done = bf16[2,4096,256]{2,1,0:T(8,128)(2,1)S(1)} copy-done((bf16[2,4096,256]{2,1,0:T(8,128)(2,1)S(1)}, bf16[2,4096,256]{2,1,0:T(8,128)(2,1)}, u32[]{:S(2)}) %copy-start) | copy-done | bytes 4194328
  9.4 0.0 copy-start.1
  9.4 1.0 %copy-done.1 = s32[8,32,512]{2,1,0:T(8,128)S(1)} copy-done((s32[8,32,512]{2,1,0:T(8,128)S(1)}, s32[8,32,512]{2,1,0:T(8,128)}, u32[]{:S(2)}) %copy-start.1) | copy-done | bytes 524312
  10.4 0.0 copy-start.3
  10.4 0.7 copy-done.3
  11.1 0.0 copy-start.5
  11.1 0.0 copy-start.6
  11.1 0.0 copy-start.4
  11.1 11.0 %fine_delays.1 = bf16[8,144,128]{2,1,0:T(8,128)(2,1)} custom-call(s32[8,32]{1,0:T(8,128)S(1)} %copy-done.3, bf16[2,4096,256]{2,1,0:T(8,128)(2,1)S(1)} %copy-done, s32[8,32,512]{2,1,0:T(8,128)S(1)} %copy-done.1), custom_call_target="tpu_custom_call" | custom-call | tf_op jit(solution)/shard_map/fine_delays/pallas_call | solution.py:174
  22.1 5.2 %all-to-all-start = ((bf16[8,144,128]{2,1,0:T(8,128)(2,1)}), bf16[8,144,128]{2,1,0:T(8,128)(2,1)S(1)}, u32[]{:S(2)}, u32[]{:S(2)}) async-start(bf16[8,144,128]{2,1,0:T(8,128)(2,1)} %fine_delays.1), calls=%async_computation | async-start | bytes 589824 | tf_op jit(solution)/shard_map/all_to_all | solution.py:194
  27.3 0.0 reduce-scatter.2.cloned.1.call-start
  27.3 0.0 copy-done.5
  27.3 0.1 copy.8.rel_ref
  27.4 0.0 copy-done.6
  27.4 0.1 copy.9.offset_ref
  27.5 7.1 %all-to-all-done.recv_ref = bf16[8,144,128]{2,1,0:T(8,128)(2,1)S(1)} async-done(((bf16[8,144,128]{2,1,0:T(8,128)(2,1)}), bf16[8,144,128]{2,1,0:T(8,128)(2,1)S(1)}, u32[]{:S(2)}, u32[]{:S(2)}) %all-to-all-start) | async-done | bytes 294944 | tf_op jit(solution)/shard_map/all_to_all | solution.py:194
  34.6 13.1 %trial_sums.1 = bf16[2048,128]{1,0:T(8,128)(2,1)} custom-call(s32[64,32]{1,0:T(8,128)S(1)} %copy.8.rel_ref, s32[64,32]{1,0:T(8,128)S(1)} %copy.9.offset_ref, bf16[8,144,128]{2,1,0:T(8,128)(2,1)S(1)} %all-to-all-done.recv_ref), custom_call_target="tpu_custom_call" | custom-call | tf_op jit(solution)/shard_map/trial_sums/pallas_call | solution.py:197
  47.7 0.0 reduce-scatter.2.cloned.1.call-update
  47.7 21.2 %reduce-scatter.2.cloned.1.call-done = bf16[512,128]{1,0:T(8,128)(2,1)} async-done(((bf16[2048,128]{1,0:T(8,128)(2,1)}), bf16[512,128]{1,0:T(8,128)(2,1)}) %reduce-scatter.2.cloned.1.call-update) | async-done | bytes 131088 | tf_op jit(solution)/shard_map/reduce_scatter | solution.py:214
  68.9 0.0 copy-done.4
  68.9 0.9 %copy-done.2 = bf16[512,128]{1,0:T(8,128)(2,1)S(1)} copy-done((bf16[512,128]{1,0:T(8,128)(2,1)S(1)}, bf16[512,128]{1,0:T(8,128)(2,1)}, u32[]{:S(2)}) %copy-start.2) | copy-done | bytes 131096
  69.8 1.3 %boxcar_peaks.1 = (bf16[2,16,2048]{2,1,0:T(8,128)(2,1)}, f32[2,16,4]{2,1,0:T(8,128)S(1)}) custom-call(s32[4]{0:T(128)S(1)} %copy-done.4, bf16[16,32,128]{2,1,0:T(8,128)(2,1)S(1)} %bitcast.1), custom_call_target="tpu_custom_call" | custom-call | tf_op jit(solution)/shard_map/boxcar_peaks/pallas_call | solution.py:216
  71.1 0.7 copy.10
  (1 shorter events, 0.0 us)
Async XLA Ops:
  7.2 2.2 %copy-start = (bf16[2,4096,256]{2,1,0:T(8,128)(2,1)S(1)}, bf16[2,4096,256]{2,1,0:T(8,128)(2,1)}, u32[]{:S(2)}) copy-start(bf16[2,4096,256]{2,1,0:T(8,128)(2,1)} %x_ref.1) | copy-start | bytes 12582916
  9.4 1.0 %copy-start.1 = (s32[8,32,512]{2,1,0:T(8,128)S(1)}, s32[8,32,512]{2,1,0:T(8,128)}, u32[]{:S(2)}) copy-start(s32[8,32,512]{2,1,0:T(8,128)} %delay_ref.1) | copy-start | bytes 1572868
  10.4 0.7 copy-start.3
  11.1 16.2 %copy-start.5 = (s32[64,32]{0,1:T(8,128)S(1)}, s32[64,32]{0,1:T(8,128)}, u32[]{:S(2)}) copy-start(s32[64,32]{0,1:T(8,128)} %param.9) | copy-start | bytes 24580
  11.1 16.3 %copy-start.6 = (s32[64,32]{0,1:T(8,128)S(1)}, s32[64,32]{0,1:T(8,128)}, u32[]{:S(2)}) copy-start(s32[64,32]{0,1:T(8,128)} %param.10) | copy-start | bytes 24580
  11.1 57.8 %copy-start.4 = (s32[4]{0:T(128)S(1)}, s32[4]{0:T(128)}, u32[]{:S(2)}) copy-start(s32[4]{0:T(128)} %width_ref.1) | copy-start | bytes 52
  22.1 12.5 %all-to-all-start = ((bf16[8,144,128]{2,1,0:T(8,128)(2,1)}), bf16[8,144,128]{2,1,0:T(8,128)(2,1)S(1)}, u32[]{:S(2)}, u32[]{:S(2)}) async-start(bf16[8,144,128]{2,1,0:T(8,128)(2,1)} %fine_delays.1), calls=%async_computation | async-start | bytes 589824 | tf_op jit(solution)/shard_map/all_to_all | solution.py:194
  27.3 41.6 %reduce-scatter.2.cloned.1.call-start = ((), (), s32[]{:S(2)}) async-start(), calls=%async_computation.2 | async-start | bytes 655360 | tf_op jit(solution)/shard_map/reduce_scatter | solution.py:214
  68.9 0.9 %copy-start.2 = (bf16[512,128]{1,0:T(8,128)(2,1)S(1)}, bf16[512,128]{1,0:T(8,128)(2,1)}, u32[]{:S(2)}) copy-start(bf16[512,128]{1,0:T(8,128)(2,1)} %reduce-scatter.2.cloned.1.call-done) | copy-start | bytes 393220
Sparse Core Ops, SparseCore 0:
  47.8 20.9 reduce-scatter.1
where the time goes:
time: 78.9 us; the launch traced here: 78.6 us
  waiting for transfers between devices  28.2 us (36%)
  Pallas kernels  25.4 us (32%)
  between operations  14.1 us (18%)
  local copies, waits for them, and re-layouts  5.66 us (7%)
  starting transfers between devices  5.21 us (7%)
    reduce_scatter x1, waiting for transfers between devices, local(): summed = lax.psum_scatter(sums, 'band', scatter_dimension=0, tiled=True)  21.2 us
    pallas_call x1, Pallas kernels, local(): pl.pallas_call(functools.partial(trial_kernel, subs, beams, bands), in_sp...  13.1 us
    pallas_call x1, Pallas kernels, local(): pl.pallas_call(functools.partial(fine_kernel, subs, sources, rows), grid_...  11 us
    all_to_all x1, waiting for transfers between devices, local(): lax.all_to_all(send, 'trial', split_axis=0, concat_axis=0, tiled=True)  7.07 us
    all_to_all x1, starting transfers between devices, local(): lax.all_to_all(send, 'trial', split_axis=0, concat_axis=0, tiled=True)  5.18 us
    unnamed x16, local copies, waits for them, and re-layouts  4.98 us
  transfers between devices with their start and end apart: 2, of which 2 were waited for; matrix products, arithmetic and copies ran while one was open for 0% of the time, Pallas kernels for 0%

commit v1 on v0

--- a/solution.py
+++ b/solution.py
@@ -69,70 +69,87 @@
             out_ref[target] = send_ref[target * rows : (target + 1) * rows].astype(jnp.bfloat16)
 
 
-def trial_kernel(subs, beams, bands, rel_ref, offset_ref, recv_ref, out_ref, flat_ref, wide_ref, sums_ref):
+def spread(subs, beams, recv_ref, wide_ref, flat_ref):
     sources, rows, _ = recv_ref.shape
-    trials = rel_ref.shape[0]
     halves = 2
     blocks = sources * halves
-    stride = wide_ref.shape[1]
     main = subs * beams * halves * QSPAN
-    lane = lax.broadcasted_iota(jnp.int32, (8, LANES), 1)
     for source in range(sources):
         flat_ref[source * rows : (source + 1) * rows] = recv_ref[source].astype(jnp.float32)
     flat_ref[sources * rows :] = jnp.zeros((rows, LANES), jnp.float32)
-    lane_all = lax.broadcasted_iota(jnp.int32, (sources, LANES), 1)
-    for sub in range(subs):
-        for beam in range(beams):
-            pair = sub * beams + beam
-            tails = flat_ref[pl.ds(rows + main + pair, sources, stride=rows), :]
-            for span in range(QSPAN):
-                row = pair * QSPAN + span
-                wide_ref[row, blocks:, :] = jnp.zeros((stride - blocks, LANES), jnp.float32)
-                for half in range(halves):
-                    piece = flat_ref[
-                        pl.ds(pair * halves * QSPAN + half * QSPAN + span, sources, stride=rows), :
-                    ]
-                    if half == halves - 1:
-                        turn = (LANES - MAXD1 - span * MAXD1) % LANES
-                        moved = pltpu.roll(tails, turn, 1) if turn else tails
-                        piece = piece + jnp.where(lane_all >= LANES - MAXD1, moved, 0.0)
-                    wide_ref[row, pl.ds(half, sources, stride=halves), :] = piece
-    first = lax.axis_index("band") * subs
-    per_band = trials // bands
-    step_rows = beams * per_band
-
-    def one_trial(trial, carry):
-        sums = [[jnp.zeros((8, LANES), jnp.float32) for _ in range(blocks // 8)] for _ in range(beams)]
+    lane = lax.broadcasted_iota(jnp.int32, (sources, LANES), 1)
+    for pair in range(subs * beams):
+        tails = flat_ref[pl.ds(rows + main + pair, sources, stride=rows), :]
+        for span in range(QSPAN):
+            row = pair * QSPAN + span
+            wide_ref[row, blocks:, :] = jnp.zeros((wide_ref.shape[1] - blocks, LANES), jnp.float32)
+            for half in range(halves):
+                place = pair * halves * QSPAN + half * QSPAN + span
+                piece = flat_ref[pl.ds(place, sources, stride=rows), :]
+                if half == halves - 1:
+                    turn = (LANES - MAXD1 - span * MAXD1) % LANES
+                    moved = pltpu.roll(tails, turn, 1) if turn else tails
+                    piece = piece + jnp.where(lane >= LANES - MAXD1, moved, 0.0)
+                wide_ref[row, pl.ds(half, sources, stride=halves), :] = piece
+
+
+def add_trials(subs, beams, first, count, place_ref, wide_ref, sums_ref):
+    blocks = sums_ref.shape[0] // (beams * count)
+    lane = lax.broadcasted_iota(jnp.int32, (8, LANES), 1)
+
+    def one_trial(inside, carry):
+        sums = [[None] * (blocks // 8) for _ in range(beams)]
         for sub in range(subs):
-            span = rel_ref[trial, first + sub]
-            shift = offset_ref[trial, first + sub]
-            coarse = shift // LANES
-            fine = shift - coarse * LANES
+            place = place_ref[sub, first + inside]
+            row = place >> 20
+            coarse = (place >> 7) & 0x1FFF
+            fine = place & (LANES - 1)
             keep = lane >= fine
-            turn = (LANES - fine) % LANES
+            turn = (LANES - fine) & (LANES - 1)
             for beam in range(beams):
-                row = (sub * beams + beam) * QSPAN + span
                 for part in range(blocks // 8):
-                    near = wide_ref[row, pl.ds(coarse + part * 8, 8), :]
-                    far = wide_ref[row, pl.ds(coarse + part * 8 + 1, 8), :]
+                    at = coarse + part * 8
+                    near = wide_ref[row + beam * QSPAN, pl.ds(at, 8), :]
+                    far = wide_ref[row + beam * QSPAN, pl.ds(at + 1, 8), :]
                     moved = pltpu.roll(jnp.where(keep, near, far), turn, 1)
-                    sums[beam][part] = sums[beam][part] + moved
-        band = trial // per_band
-        inside = trial - band * per_band
+                    held = sums[beam][part]
+                    sums[beam][part] = moved if held is None else held + moved
         for beam in range(beams):
             for part in range(blocks // 8):
-                start = (band * blocks + part * 8) * step_rows + beam * per_band + inside
-                sums_ref[pl.ds(start, 8, stride=step_rows), :] = sums[beam][part]
+                start = part * 8 * beams * count + beam * count + inside
+                sums_ref[pl.ds(start, 8, stride=beams * count), :] = sums[beam][part]
         return carry
 
-    lax.fori_loop(0, trials, one_trial, 0)
-    out_ref[...] = sums_ref[...].astype(jnp.bfloat16)
-
-
-def peak_kernel(beams, scale, width_ref, x_ref, series_ref, peak_ref):
-    blocks, rows, _ = x_ref.shape
+    lax.fori_loop(0, count, one_trial, 0, unroll=2)
+
+
+def partner(place, step, peers):
+    return place ^ step if peers & (peers - 1) == 0 else (place + step) % peers
+
+
+def first_kernel(subs, beams, bands, step, count, place_ref, recv_ref, wide_ref, out_ref, flat_ref, sums_ref):
+    spread(subs, beams, recv_ref, wide_ref, flat_ref)
+    band = partner(lax.axis_index("band"), step, bands)
+    add_trials(subs, beams, band * count, count, place_ref, wide_ref, sums_ref)
+    out_ref[...] = sums_ref[...].reshape(out_ref.shape).astype(out_ref.dtype)
+
+
+def next_kernel(subs, beams, bands, step, count, place_ref, wide_ref, out_ref, sums_ref):
+    band = partner(lax.axis_index("band"), step, bands)
+    add_trials(subs, beams, band * count, count, place_ref, wide_ref, sums_ref)
+    out_ref[...] = sums_ref[...].reshape(out_ref.shape).astype(out_ref.dtype)
+
+
+def peak_kernel(beams, scale, width_ref, *refs):
+    x_refs, (series_ref, peak_ref) = refs[:-2], refs[-2:]
+    blocks, rows, _ = x_refs[0].shape
     per_beam = rows // beams
-    series = [(x_ref[block].astype(jnp.float32) / scale).astype(jnp.bfloat16) for block in range(blocks)]
+    series = []
+    for block in range(blocks):
+        total = x_refs[0][block].astype(jnp.float32)
+        for x_ref in x_refs[1:]:
+            total = total + x_ref[block].astype(jnp.float32)
+        series.append((total / scale).astype(jnp.bfloat16))
     for block in range(blocks):
         for beam in range(beams):
             series_ref[beam, :, block * LANES : (block + 1) * LANES] = (
@@ -188,45 +205,58 @@
             ],
         ),
         out_shape=jax.ShapeDtypeStruct((sources, rows, LANES), jnp.bfloat16),
-        compiler_params=pltpu.CompilerParams(vmem_limit_bytes=48 << 20),
         name="fine_delays",
     )(span_start, intensity, fine_delay)
+    own = lax.axis_index("band") * subs
+    own_rel = lax.dynamic_slice_in_dim(sub_rel.T, own, subs, 0)
+    own_shift = lax.dynamic_slice_in_dim(offset.T, own, subs, 0)
+    pair = jnp.arange(subs, dtype=jnp.int32)[:, None] * beams
+    places = ((pair * QSPAN + own_rel) << 20) + own_shift
     received = lax.all_to_all(send, "trial", split_axis=0, concat_axis=0, tiled=True)
     stride = round_up(blocks + length // 2 // LANES + 1, 8)
-    per_band = trials // bands
-    sums = pl.pallas_call(
-        functools.partial(trial_kernel, subs, beams, bands),
-        in_specs=[
-            pl.BlockSpec(memory_space=pltpu.SMEM),
-            pl.BlockSpec(memory_space=pltpu.SMEM),
-            pl.BlockSpec(memory_space=pltpu.VMEM),
-        ],
-        out_specs=pl.BlockSpec(memory_space=pltpu.VMEM),
-        scratch_shapes=[
-            pltpu.VMEM(((sources + 1) * rows, LANES), jnp.float32),
-            pltpu.VMEM((subs * beams * QSPAN, stride, LANES), jnp.float32),
-            pltpu.VMEM((blocks * beams * trials, LANES), jnp.float32),
-        ],
-        out_shape=jax.ShapeDtypeStruct((blocks * beams * trials, LANES), jnp.bfloat16),
-        compiler_params=pltpu.CompilerParams(vmem_limit_bytes=48 << 20),
-        name="trial_sums",
-    )(sub_rel, offset, received)
-    summed = lax.psum_scatter(sums, "band", scatter_dimension=0, tiled=True)
-    summed = summed.reshape(blocks, beams * per_band, LANES)
+    count = trials // bands
+    in_smem = pl.BlockSpec(memory_space=pltpu.SMEM)
+    in_vmem = pl.BlockSpec(memory_space=pltpu.VMEM)
+    wide_shape = (subs * beams * QSPAN, stride, LANES)
+    chunk_shape = (blocks, beams * count, LANES)
+    sums_scratch = pltpu.VMEM((blocks * beams * count, LANES), jnp.float32)
+    steps = list(range(bands - 1, 0, -1))
+    wide = None
+    arrived = []
+    for step in steps + [0]:
+        chunk = jax.ShapeDtypeStruct(chunk_shape, jnp.bfloat16 if step else jnp.float32)
+        if wide is None:
+            wide, sums = pl.pallas_call(
+                functools.partial(first_kernel, subs, beams, bands, step, count),
+                in_specs=[in_smem, in_vmem],
+                out_specs=[in_vmem, in_vmem],
+                scratch_shapes=[pltpu.VMEM(((sources + 1) * rows, LANES), jnp.float32), sums_scratch],
+                out_shape=[jax.ShapeDtypeStruct(wide_shape, jnp.float32), chunk],
+                name="spread_and_add",
+            )(places, received)
+        else:
+            sums = pl.pallas_call(
+                functools.partial(next_kernel, subs, beams, bands, step, count),
+                in_specs=[in_smem, in_vmem],
+                out_specs=in_vmem,
+                scratch_shapes=[sums_scratch],
+                out_shape=chunk,
+                name="add_trials",
+            )(places, wide)
+        if step:
+            pairs = [(place, partner(place, step, bands)) for place in range(bands)]
+            sums = lax.ppermute(sums, "band", pairs)
+        arrived.append(sums)
     return pl.pallas_call(
         functools.partial(peak_kernel, beams, math.sqrt(channels * bands)),
-        in_specs=[
-            pl.BlockSpec(memory_space=pltpu.SMEM),
-            pl.BlockSpec(memory_space=pltpu.VMEM),
+        in_specs=[in_smem] + [in_vmem] * bands,
+        out_specs=[in_vmem] * 2,
+        out_shape=[
+            jax.ShapeDtypeStruct((beams, count, length), jnp.bfloat16),
+            jax.ShapeDtypeStruct((beams, count, widths.shape[0]), jnp.float32),
         ],
-        out_specs=[pl.BlockSpec(memory_space=pltpu.VMEM)] * 2,
-        out_shape=[
-            jax.ShapeDtypeStruct((beams, per_band, length), jnp.bfloat16),
-            jax.ShapeDtypeStruct((beams, per_band, widths.shape[0]), jnp.float32),
-        ],
-        compiler_params=pltpu.CompilerParams(vmem_limit_bytes=48 << 20),
         name="boxcar_peaks",
-    )(widths, summed)
+    )(widths, *arrived[::-1])
 
 
 def solution(mesh):

time: 78.9 us -> 54.8 us (0.69)
  waiting for transfers between devices: 28.2 us -> 12.2 us
  between operations: 14.1 us -> 0.65 us
  starting transfers between devices: 5.21 us -> 9.56 us
  local copies, waits for them, and re-layouts: 5.66 us -> 3.45 us
  Pallas kernels: 25.4 us -> 27.1 us
  other arithmetic: 0 us -> 1.38 us
    reduce_scatter x1 -> x0, waiting for transfers between devices: 21.2 us -> none  [local(): summed = lax.psum_scatter(sums, 'band', scatter_dimension=0, tiled=True)]
    ppermute x0 -> x3, waiting for transfers between devices: none -> 6.27 us  [local(): sums = lax.ppermute(sums, 'band', pairs)]
    ppermute x0 -> x3, starting transfers between devices: none -> 4.39 us  [local(): sums = lax.ppermute(sums, 'band', pairs)]
    unnamed x16 -> x8, local copies, waits for them, and re-layouts: 4.98 us -> 2.06 us
    add x0 -> x1, other arithmetic: none -> 1.37 us  [local(): places = (pair * QSPAN + own_rel << 20) + own_shift]
    all_to_all x1, waiting for transfers between devices: 7.07 us -> 5.9 us  [local(): lax.all_to_all(send, 'trial', split_axis=0, concat_axis=0, tiled=True)]
    pallas_call x1, Pallas kernels: 1.3 us -> 2.26 us  [local(): pl.pallas_call(functools.partial(peak_kernel, beams, math.sqrt(channels *...]
    pallas_call x1, Pallas kernels: 11 us -> 11.9 us  [local(): pl.pallas_call(functools.partial(fine_kernel, subs, sources, rows), grid_...]
  transfers between devices with their start and end apart: 2 -> 4, of which waited for: 2 -> 2; matrix products, arithmetic and copies ran while one was open for 0% -> 3% of each run, Pallas kernels for 0% -> 6%
where the time goes in v1:
time: 54.8 us; the launch traced here: 54.3 us
  Pallas kernels  27.1 us (49%)
  waiting for transfers between devices  12.2 us (22%)
  starting transfers between devices  9.56 us (17%)
  local copies, waits for them, and re-layouts  3.45 us (6%)
  other arithmetic  1.38 us (3%)
  between operations  0.65 us (1%)
    pallas_call x1, Pallas kernels, local(): pl.pallas_call(functools.partial(fine_kernel, subs, sources, rows), grid_...  11.9 us
    pallas_call x3, Pallas kernels, local(): pl.pallas_call(functools.partial(next_kernel, subs, beams, bands, step, c...  9.53 us
    ppermute x3, waiting for transfers between devices, local(): sums = lax.ppermute(sums, 'band', pairs)  6.27 us
    all_to_all x1, waiting for transfers between devices, local(): lax.all_to_all(send, 'trial', split_axis=0, concat_axis=0, tiled=True)  5.9 us
    all_to_all x1, starting transfers between devices, local(): lax.all_to_all(send, 'trial', split_axis=0, concat_axis=0, tiled=True)  5.18 us
    ppermute x3, starting transfers between devices, local(): sums = lax.ppermute(sums, 'band', pairs)  4.39 us
    pallas_call x1, Pallas kernels, local(): pl.pallas_call(functools.partial(first_kernel, subs, beams, bands, step,...  3.36 us
    pallas_call x1, Pallas kernels, local(): pl.pallas_call(functools.partial(peak_kernel, beams, math.sqrt(channels *...  2.26 us
  transfers between devices with their start and end apart: 4, of which 2 were waited for; matrix products, arithmetic and copies ran while one was open for 3% of the time, Pallas kernels for 6%

profile of v1, /device:TPU:0, one launch (start us, length us, event | category | flops | bytes accessed | tf_op | source)
XLA Modules:
  0.0 54.3 jit_solution(2179815012181746182)
XLA Ops:
  0.6 11.9 %fine_delays.1 = bf16[8,144,128]{2,1,0:T(8,128)(2,1)} custom-call(s32[8,32]{1,0:T(8,128)} %span_ref.1, bf16[2,4096,256]{2,1,0:T(8,128)(2,1)} %x_ref.1, s32[8,32,512]{2,1,0:T(8,128)} %delay_ref.1), custom_call_target="tpu_custom_call" | custom-call | tf_op jit(solution)/shard_map/fine_delays/pallas_call | solution.py:191
  12.6 5.2 %all-to-all-start = ((bf16[8,144,128]{2,1,0:T(8,128)(2,1)}), bf16[8,144,128]{2,1,0:T(8,128)(2,1)S(1)}, u32[]{:S(2)}, u32[]{:S(2)}) async-start(bf16[8,144,128]{2,1,0:T(8,128)(2,1)} %fine_delays.1), calls=%async_computation | async-start | bytes 589824 | tf_op jit(solution)/shard_map/all_to_all | solution.py:215
  17.8 1.4 %add_bitcast_fusion.place_ref = s32[8,64]{1,0:T(8,128)} fusion(s32[64,32]{0,1:T(8,128)} %param.10, s32[]{:T(128)S(6)} %select_n.4, s32[64,32]{0,1:T(8,128)} %param.9, s32[8]{0:T(128)S(1)} %iota_multiply_fusion), kind=kLoop, calls=%fused_computation | loop fusion | flops 1536 | bytes 6180 | tf_op jit(solution)/shard_map/add | solution.py:214
  19.1 5.9 %all-to-all-done.recv_ref = bf16[8,144,128]{2,1,0:T(8,128)(2,1)S(1)} async-done(((bf16[8,144,128]{2,1,0:T(8,128)(2,1)}), bf16[8,144,128]{2,1,0:T(8,128)(2,1)S(1)}, u32[]{:S(2)}, u32[]{:S(2)}) %all-to-all-start) | async-done | bytes 294944 | tf_op jit(solution)/shard_map/all_to_all | solution.py:215
  25.0 0.0 copy-start
  25.0 0.7 %copy-done = bf16[8,144,128]{2,1,0:T(8,128)(2,1)} copy-done((bf16[8,144,128]{2,1,0:T(8,128)(2,1)}, bf16[8,144,128]{2,1,0:T(8,128)(2,1)S(1)}, u32[]{:S(2)}) %copy-start) | copy-done | bytes 294936
  25.8 3.4 %spread_and_add.1 = (f32[64,32,128]{2,1,0:T(8,128)}, bf16[16,32,128]{2,1,0:T(8,128)(2,1)}) custom-call(s32[8,64]{1,0:T(8,128)} %add_bitcast_fusion.place_ref, bf16[8,144,128]{2,1,0:T(8,128)(2,1)} %copy-done), custom_call_target="tpu_custom_call" | custom-call | tf_op jit(solution)/shard_map/spread_and_add/pallas_call | solution.py:229
  29.2 3.1 %add_trials.5 = bf16[16,32,128]{2,1,0:T(8,128)(2,1)} custom-call(s32[8,64]{1,0:T(8,128)} %add_bitcast_fusion.place_ref, f32[64,32,128]{2,1,0:T(8,128)} %get-tuple-element.4.wide_ref), custom_call_target="tpu_custom_call" | custom-call | tf_op jit(solution)/shard_map/add_trials/pallas_call | solution.py:238
  32.3 3.2 %add_trials.4 = bf16[16,32,128]{2,1,0:T(8,128)(2,1)} custom-call(s32[8,64]{1,0:T(8,128)} %add_bitcast_fusion.place_ref, f32[64,32,128]{2,1,0:T(8,128)} %get-tuple-element.4.wide_ref), custom_call_target="tpu_custom_call" | custom-call | tf_op jit(solution)/shard_map/add_trials/pallas_call | solution.py:238
  35.5 1.6 %collective-permute-start = (bf16[16,32,128]{2,1,0:T(8,128)(2,1)}, bf16[16,32,128]{2,1,0:T(8,128)(2,1)S(1)}, u32[]{:S(2)}, u32[]{:S(2)}) collective-permute-start(bf16[16,32,128]{2,1,0:T(8,128)(2,1)} %add_trials.4), channel_id=1, source_target_pairs={{0,8},{8,0},{16,24},{24,16},{1,9},{9,1},{17,25},{25,17},{2,10},{10... | collective-permute-start | bytes 393224 | tf_op jit(solution)/shard_map/ppermute | solution.py:248
  37.0 2.6 %collective-permute-start.1 = (bf16[16,32,128]{2,1,0:T(8,128)(2,1)}, bf16[16,32,128]{2,1,0:T(8,128)(2,1)S(1)}, u32[]{:S(2)}, u32[]{:S(2)}) collective-permute-start(bf16[16,32,128]{2,1,0:T(8,128)(2,1)} %add_trials.5), channel_id=1, source_target_pairs={{0,16},{8,24},{16,0},{24,8},{1,17},{9,25},{17,1},{25,9},{2,18},{10... | collective-permute-start | bytes 393224 | tf_op jit(solution)/shard_map/ppermute | solution.py:248
  39.6 0.2 collective-permute-start.2
  39.8 3.2 %add_trials.3.refs_0_ = f32[16,32,128]{2,1,0:T(8,128)} custom-call(s32[8,64]{1,0:T(8,128)} %add_bitcast_fusion.place_ref, f32[64,32,128]{2,1,0:T(8,128)} %get-tuple-element.4.wide_ref), custom_call_target="tpu_custom_call" | custom-call | tf_op jit(solution)/shard_map/add_trials/pallas_call | solution.py:238
  43.1 0.0 collective-permute-done.refs_1_
  43.1 0.0 copy-start.1
  43.1 6.3 %collective-permute-done.1.refs_2_ = bf16[16,32,128]{2,1,0:T(8,128)(2,1)S(1)} collective-permute-done((bf16[16,32,128]{2,1,0:T(8,128)(2,1)}, bf16[16,32,128]{2,1,0:T(8,128)(2,1)S(1)}, u32[]{:S(2)}, u32[]{:S(2)}) %collective-permute-start.1) | collective-permute-done | bytes 131104 | tf_op jit(solution)/shard_map/ppermute | solution.py:248
  49.3 0.0 copy-start.2
  49.3 0.0 collective-permute-done.2.refs_3_
  49.3 0.0 copy-done.1
  49.3 0.7 %copy-done.2 = bf16[16,32,128]{2,1,0:T(8,128)(2,1)} copy-done((bf16[16,32,128]{2,1,0:T(8,128)(2,1)}, bf16[16,32,128]{2,1,0:T(8,128)(2,1)S(1)}, u32[]{:S(2)}) %copy-start.2) | copy-done | bytes 131096
  50.0 0.0 copy-start.3
  50.0 0.7 %copy-done.3 = bf16[16,32,128]{2,1,0:T(8,128)(2,1)} copy-done((bf16[16,32,128]{2,1,0:T(8,128)(2,1)}, bf16[16,32,128]{2,1,0:T(8,128)(2,1)S(1)}, u32[]{:S(2)}) %copy-start.3) | copy-done | bytes 131096
  50.7 2.3 %boxcar_peaks.1 = (bf16[2,16,2048]{2,1,0:T(8,128)(2,1)}, f32[2,16,4]{2,1,0:T(8,128)}) custom-call(s32[4]{0:T(128)} %width_ref.1, f32[16,32,128]{2,1,0:T(8,128)} %add_trials.3.refs_0_, bf16[16,32,128]{2,1,0:T(8,128)(2,1)} %copy-done.1, bf16[16,32,128]{2,1,0:T(8,128)(2,1)} %copy-done.2, bf16[16,32,128]{2,1,0:T(8,128)(2,1)} %copy-done.3), custom_call_target="tpu_custom_call" | custom-call | tf_op jit(solution)/shard_map/boxcar_peaks/pallas_call | solution.py:250
  52.9 1.4 %copy.8 = f32[2,16,4]{1,2,0:T(4,128)} copy(f32[2,16,4]{2,1,0:T(8,128)} %get-tuple-element.7) | data formatting | bytes 1024 | tf_op jit(solution)/shard_map/boxcar_peaks/pallas_call | solution.py:250
  (1 shorter events, 0.0 us)
Async XLA Ops:
  12.6 12.5 %all-to-all-start = ((bf16[8,144,128]{2,1,0:T(8,128)(2,1)}), bf16[8,144,128]{2,1,0:T(8,128)(2,1)S(1)}, u32[]{:S(2)}, u32[]{:S(2)}) async-start(bf16[8,144,128]{2,1,0:T(8,128)(2,1)} %fine_delays.1), calls=%async_computation | async-start | bytes 589824 | tf_op jit(solution)/shard_map/all_to_all | solution.py:215
  25.0 0.7 %copy-start = (bf16[8,144,128]{2,1,0:T(8,128)(2,1)}, bf16[8,144,128]{2,1,0:T(8,128)(2,1)S(1)}, u32[]{:S(2)}) copy-start(bf16[8,144,128]{2,1,0:T(8,128)(2,1)S(1)} %all-to-all-done.recv_ref) | copy-start | bytes 884740
  35.5 7.6 %collective-permute-start = (bf16[16,32,128]{2,1,0:T(8,128)(2,1)}, bf16[16,32,128]{2,1,0:T(8,128)(2,1)S(1)}, u32[]{:S(2)}, u32[]{:S(2)}) collective-permute-start(bf16[16,32,128]{2,1,0:T(8,128)(2,1)} %add_trials.4), channel_id=1, source_target_pairs={{0,8},{8,0},{16,24},{24,16},{1,9},{9,1},{17,25},{25,17},{2,10},{10... | collective-permute-start | bytes 393224 | tf_op jit(solution)/shard_map/ppermute | solution.py:248
  37.0 12.3 %collective-permute-start.1 = (bf16[16,32,128]{2,1,0:T(8,128)(2,1)}, bf16[16,32,128]{2,1,0:T(8,128)(2,1)S(1)}, u32[]{:S(2)}, u32[]{:S(2)}) collective-permute-start(bf16[16,32,128]{2,1,0:T(8,128)(2,1)} %add_trials.5), channel_id=1, source_target_pairs={{0,16},{8,24},{16,0},{24,8},{1,17},{9,25},{17,1},{25,9},{2,18},{10... | collective-permute-start | bytes 393224 | tf_op jit(solution)/shard_map/ppermute | solution.py:248
  39.6 9.7 %collective-permute-start.2 = (bf16[16,32,128]{2,1,0:T(8,128)(2,1)}, bf16[16,32,128]{2,1,0:T(8,128)(2,1)S(1)}, u32[]{:S(2)}, u32[]{:S(2)}) collective-permute-start(bf16[16,32,128]{2,1,0:T(8,128)(2,1)} %get-tuple-element.5), channel_id=1, source_target_pairs={{0,24},{8,16},{16,8},{24,0},{1,25},{9,17},{17,9},{25,1},{2,26},{10... | collective-permute-start | bytes 393224 | tf_op jit(solution)/shard_map/ppermute | solution.py:248
  43.1 6.3 %copy-start.1 = (bf16[16,32,128]{2,1,0:T(8,128)(2,1)}, bf16[16,32,128]{2,1,0:T(8,128)(2,1)S(1)}, u32[]{:S(2)}) copy-start(bf16[16,32,128]{2,1,0:T(8,128)(2,1)S(1)} %collective-permute-done.refs_1_) | copy-start | bytes 393220
  49.3 0.7 %copy-start.2 = (bf16[16,32,128]{2,1,0:T(8,128)(2,1)}, bf16[16,32,128]{2,1,0:T(8,128)(2,1)S(1)}, u32[]{:S(2)}) copy-start(bf16[16,32,128]{2,1,0:T(8,128)(2,1)S(1)} %collective-permute-done.1.refs_2_) | copy-start | bytes 393220
  50.0 0.7 %copy-start.3 = (bf16[16,32,128]{2,1,0:T(8,128)(2,1)}, bf16[16,32,128]{2,1,0:T(8,128)(2,1)S(1)}, u32[]{:S(2)}) copy-start(bf16[16,32,128]{2,1,0:T(8,128)(2,1)S(1)} %collective-permute-done.2.refs_3_) | copy-start | bytes 393220

commit v2 on v1

v2 whole, which is shorter than its diff:
```python
import functools
import math

import jax
import jax.numpy as jnp
from jax import lax
from jax.experimental import pallas as pl
from jax.experimental.pallas import tpu as pltpu
from jax.sharding import PartitionSpec as P

QSPAN = 4
MAXD1 = 32
LANES = 128


def round_up(number, step):
    return (number + step - 1) // step * step


def fine_kernel(trial_ranges, span_ref, x_hbm, delay_ref, out_ref, x_ref, lagged_ref, joined_ref, tail_ref, sems):
    subs, beams, width, block_len = x_ref.shape
    q_count = delay_ref.shape[1]
    packed = LANES // q_count
    tiles = MAXD1 // packed
    halves = block_len // LANES
    reach = MAXD1 + block_len
    unit = trial_ranges * QSPAN * packed
    per_range = QSPAN * packed
    copies = [
        pltpu.make_async_copy(x_hbm.at[:, pl.ds(sub * width, width), :], x_ref.at[sub], sems.at[sub])
        for sub in range(subs)
    ]
    for copy in copies:
        copy.start()
    for beam in range(beams):
        lagged_ref[beam, :MAXD1, :] = jnp.zeros((MAXD1, MAXD1 * q_count), jnp.float32)
        lagged_ref[beam, reach:, :] = jnp.zeros((MAXD1, MAXD1 * q_count), jnp.float32)
    joined_ref[:, :, reach:, :] = jnp.zeros((packed, beams, 8, LANES), jnp.float32)
    own = lax.axis_index("band") * subs
    lane = lax.broadcasted_iota(jnp.int32, (8, LANES), 1)
    row_id = lax.broadcasted_iota(jnp.int32, (QSPAN * packed, LANES), 0)
    lane_id = lax.broadcasted_iota(jnp.int32, (QSPAN * packed, LANES), 1)
    tail_row = lax.broadcasted_iota(jnp.int32, (trial_ranges * packed, LANES), 0)
    tail_lane = lax.broadcasted_iota(jnp.int32, (trial_ranges * packed, LANES), 1)
    for group in range(subs // packed):
        for place in range(packed):
            sub = group * packed + place
            tiled = jnp.concatenate([delay_ref[sub]] * packed, axis=0).astype(jnp.float32).T
            tiled = tiled - (lax.broadcasted_iota(jnp.int32, tiled.shape, 1) // q_count).astype(jnp.float32)
            selector = jnp.concatenate([jnp.where(tiled == jnp.float32(tile * packed), 1.0, 0.0).astype(jnp.bfloat16) for tile in range(tiles)], axis=1)
            copies[sub].wait()
            for beam in range(beams):
                lagged_ref[beam, MAXD1:reach, :] = lax.dot_general(
                    x_ref[sub, beam], selector, (((0,), (0,)), ((), ())), preferred_element_type=jnp.float32
                )
                for start in range(0, reach, 8):
                    total = lagged_ref[beam, start : start + 8, :LANES]
                    for tile in range(1, tiles):
                        at = start + packed * tile
                        total = total + lagged_ref[beam, at : at + 8, tile * LANES : (tile + 1) * LANES]
                    joined_ref[place, beam, start : start + 8, :] = total
        firsts = [[span_ref[target, own + group * packed + place] for place in range(packed)] for target in range(trial_ranges)]
        chooser = []
        for target in range(trial_ranges):
            column = jnp.zeros((per_range, LANES), jnp.int32)
            for place in range(packed):
                column = jnp.where(row_id % packed == place, firsts[target][place] + place * q_count, column)
            chooser.append((lane_id == column + row_id // packed).astype(jnp.float32))
        chooser = jnp.concatenate(chooser, axis=0).astype(jnp.bfloat16)
        tail_column = jnp.zeros((trial_ranges * packed, LANES), jnp.int32)
        for target in range(trial_ranges):
            for place in range(packed):
                tail_column = jnp.where(tail_row == target * packed + place, firsts[target][place] + place * q_count, tail_column)
        tail_chooser = jnp.concatenate([(tail_lane == tail_column + span).astype(jnp.float32) for span in range(QSPAN)], axis=0).astype(jnp.bfloat16)
        for beam in range(beams):
            pieces = []
            for start in list(range(MAXD1, reach, 8)) + list(range(0, MAXD1, 8)):
                total = None
                for turn in range(packed):
                    mixed = None
                    for part in range(packed):
                        there = (part + turn) % packed
                        piece = joined_ref[there, beam, start + part : start + part + 8, :]
                        mixed = piece if mixed is None else jnp.where(lane >= part * q_count, piece, mixed)
                    if turn:
                        mixed = pltpu.roll(mixed, turn * q_count, 1)
                    total = mixed if total is None else total + mixed
                pieces.append(total)
            rows = jnp.concatenate(pieces, axis=0).astype(jnp.bfloat16)
            chosen = lax.dot_general(
                chooser, rows[:block_len], (((1,), (1,)), ((), ())), preferred_element_type=jnp.float32
            ).astype(jnp.bfloat16)
            for target in range(trial_ranges):
                for half in range(halves):
                    at = ((group * beams + beam) * halves + half) * per_range
                    out_ref[target, at : at + per_range, :] = chosen[
                        target * per_range : (target + 1) * per_range, half * LANES : (half + 1) * LANES
                    ]
            tails = lax.dot_general(
                tail_chooser, rows[block_len:], (((1,), (1,)), ((), ())), preferred_element_type=jnp.float32
            )
            step = trial_ranges * packed
            tails = jnp.concatenate([tails[span * step : (span + 1) * step] for span in range(QSPAN)], axis=1)
            for target in range(trial_ranges):
                tail_ref[target, pl.ds((group * beams + beam) * packed, packed), :] = tails[target * packed : (target + 1) * packed]
    main = subs * beams * halves * QSPAN
    for target in range(trial_ranges):
        out_ref[target, main:, :] = tail_ref[target].astype(jnp.bfloat16)


def spread(subs, beams, packed, recv_ref, wide_ref, flat_ref):
    sources, rows, _ = recv_ref.shape
    halves = 2
    blocks = sources * halves
    main = subs * beams * halves * QSPAN
    for source in range(sources):
        flat_ref[source * rows : (source + 1) * rows] = recv_ref[source].astype(jnp.float32)
    flat_ref[sources * rows :] = jnp.zeros((rows, LANES), jnp.float32)
    lane = lax.broadcasted_iota(jnp.int32, (sources, LANES), 1)
    for pair in range(subs * beams):
        sub, beam = pair // beams, pair % beams
        group, inside = sub // packed, sub % packed
        tail_at = main + (group * beams + beam) * packed + inside
        tails = flat_ref[pl.ds(rows + tail_at, sources, stride=rows), :]
        for span in range(QSPAN):
            row = pair * QSPAN + span
            wide_ref[row, blocks:, :] = jnp.zeros((wide_ref.shape[1] - blocks, LANES), jnp.float32)
            for half in range(halves):
                place = (((group * beams + beam) * halves + half) * QSPAN + span) * packed + inside
                piece = flat_ref[pl.ds(place, sources, stride=rows), :]
                if half == halves - 1:
                    turn = (LANES - MAXD1 - span * MAXD1) % LANES
                    moved = pltpu.roll(tails, turn, 1) if turn else tails
                    piece = piece + jnp.where(lane >= LANES - MAXD1, moved, 0.0)
                wide_ref[row, pl.ds(half, sources, stride=halves), :] = piece


def add_trials(subs, beams, first, count, place_ref, wide_ref, sums_ref, out_ref):
    blocks = sums_ref.shape[0] // (beams * count)
    lane = lax.broadcasted_iota(jnp.int32, (8, LANES), 1)

    def one_trial(inside, carry):
        sums = [[None] * (blocks // 8) for _ in range(beams)]
        for sub in range(subs):
            place = place_ref[sub, first + inside]
            row = place >> 20
            coarse = (place >> 7) & 0x1FFF
            fine = place & (LANES - 1)
            keep = lane >= fine
            turn = (LANES - fine) & (LANES - 1)
            for beam in range(beams):
                for part in range(blocks // 8):
                    at = coarse + part * 8
                    near = wide_ref[row + beam * QSPAN, pl.ds(at, 8), :]
                    far = wide_ref[row + beam * QSPAN, pl.ds(at + 1, 8), :]
                    moved = pltpu.roll(jnp.where(keep, near, far), turn, 1)
                    held = sums[beam][part]
                    sums[beam][part] = moved if held is None else held + moved
        for beam in range(beams):
            for part in range(blocks // 8):
                start = part * 8 * beams * count + beam * count + inside
                sums_ref[pl.ds(start, 8, stride=beams * count), :] = sums[beam][part]
        return carry

    lax.fori_loop(0, count, one_trial, 0, unroll=min(count, 8))
    out_ref[...] = sums_ref[...].reshape(out_ref.shape).astype(out_ref.dtype)


def partner(place, step, peers):
    return place ^ step if peers & (peers - 1) == 0 else (place + step) % peers


def first_kernel(subs, beams, packed, bands, step, count, place_ref, recv_ref, wide_ref, out_ref, flat_ref, sums_ref):
    spread(subs, beams, packed, recv_ref, wide_ref, flat_ref)
    band = partner(lax.axis_index("band"), step, bands)
    add_trials(subs, beams, band * count, count, place_ref, wide_ref, sums_ref, out_ref)


def next_kernel(subs, beams, bands, steps, count, place_ref, wide_ref, *refs):
    for step, out_ref in zip(steps, refs):
        band = partner(lax.axis_index("band"), step, bands)
        add_trials(subs, beams, band * count, count, place_ref, wide_ref, refs[-1], out_ref)


def peak_kernel(beams, scale, width_ref, *refs):
    x_refs, (series_ref, peak_ref) = refs[:-2], refs[-2:]
    blocks, rows, _ = x_refs[0].shape
    per_beam = rows // beams
    series = []
    for block in range(blocks):
        total = x_refs[0][block].astype(jnp.float32)
        for x_ref in x_refs[1:]:
            total = total + x_ref[block].astype(jnp.float32)
        series.append((total / scale).astype(jnp.bfloat16))
    for block in range(blocks):
        for beam in range(beams):
            series_ref[beam, :, block * LANES : (block + 1) * LANES] = (
                series[block].astype(jnp.float32)[beam * per_beam : (beam + 1) * per_beam].astype(jnp.bfloat16)
            )
    following = series[1:] + [jnp.zeros_like(series[0])]
    left = jnp.concatenate(
        [jnp.concatenate([here, after], axis=1) for here, after in zip(series, following)], axis=0
    )
    source = lax.broadcasted_iota(jnp.int32, (2 * LANES, LANES), 0)
    place = lax.broadcasted_iota(jnp.int32, (2 * LANES, LANES), 1)
    for slot in range(peak_ref.shape[1]):
        width = width_ref[slot]
        window = ((source >= place) & (source < place + width)).astype(jnp.bfloat16)
        totals = jnp.dot(left, window, preferred_element_type=jnp.float32)
        best = totals[:rows]
        for block in range(1, blocks):
            best = jnp.maximum(best, totals[block * rows : (block + 1) * rows])
        root = jnp.sqrt(jnp.full((1, rows), width, jnp.int32).astype(jnp.float32))
        peaks = jnp.max(best.T, axis=0, keepdims=True) / root
        for beam in range(beams):
            peak_ref[beam, slot : slot + 1, :] = peaks[:, beam * per_beam : (beam + 1) * per_beam]


def local(intensity, fine_delay, span_start, sub_rel, offset, widths):
    beams, channels, block_len = intensity.shape
    subs, q_count, width = fine_delay.shape
    sources = lax.axis_size("trial")
    bands = lax.axis_size("band")
    trials = sub_rel.shape[0]
    halves = block_len // LANES
    packed = LANES // q_count
    blocks = sources * halves
    length = sources * block_len
    main = subs * beams * halves * QSPAN
    rows = round_up(main + subs * beams, 16)
    in_smem = pl.BlockSpec(memory_space=pltpu.SMEM)
    in_vmem = pl.BlockSpec(memory_space=pltpu.VMEM)
    small = pltpu.CompilerParams(vmem_limit_bytes=16 << 20)
    send = pl.pallas_call(
        functools.partial(fine_kernel, sources),
        in_specs=[in_smem, pl.BlockSpec(memory_space=pl.ANY), in_vmem],
        out_specs=in_vmem,
        scratch_shapes=[
            pltpu.VMEM((subs, beams, width, block_len), jnp.bfloat16),
            pltpu.VMEM((beams, block_len + 2 * MAXD1, MAXD1 * q_count), jnp.float32),
            pltpu.VMEM((packed, beams, block_len + MAXD1 + 8, LANES), jnp.float32),
            pltpu.VMEM((sources, rows - main, LANES), jnp.float32),
            pltpu.SemaphoreType.DMA((subs,)),
        ],
        out_shape=jax.ShapeDtypeStruct((sources, rows, LANES), jnp.bfloat16),
        compiler_params=pltpu.CompilerParams(vmem_limit_bytes=61 << 20),
        name="fine_delays",
    )(span_start, intensity, fine_delay)
    own = lax.axis_index("band") * subs
    own_rel = lax.dynamic_slice_in_dim(sub_rel.T, own, subs, 0)
    own_shift = lax.dynamic_slice_in_dim(offset.T, own, subs, 0)
    pair = jnp.arange(subs, dtype=jnp.int32)[:, None] * beams
    places = ((pair * QSPAN + own_rel) << 20) + own_shift
    received = lax.all_to_all(send, "trial", split_axis=0, concat_axis=0, tiled=True)
    stride = round_up(blocks + length // 2 // LANES + 1, 8)
    count = trials // bands
    chunk_shape = (blocks, beams * count, LANES)
    sums_scratch = pltpu.VMEM((blocks * beams * count, LANES), jnp.float32)
    steps = list(range(bands - 1, -1, -1))
    chunks = [jax.ShapeDtypeStruct(chunk_shape, jnp.bfloat16 if step else jnp.float32) for step in steps]
    wide, first = pl.pallas_call(
        functools.partial(first_kernel, subs, beams, packed, bands, steps[0], count),
        in_specs=[in_smem, in_vmem],
        out_specs=[in_vmem, in_vmem],
        scratch_shapes=[pltpu.VMEM(((sources + 1) * rows, LANES), jnp.float32), sums_scratch],
        out_shape=[jax.ShapeDtypeStruct((subs * beams * QSPAN, stride, LANES), jnp.float32), chunks[0]],
        compiler_params=small,
        name="spread_and_add",
    )(places, received)
    rest = pl.pallas_call(
        functools.partial(next_kernel, subs, beams, bands, steps[1:], count),
        in_specs=[in_smem, in_vmem],
        out_specs=[in_vmem] * (bands - 1),
        scratch_shapes=[sums_scratch],
        out_shape=chunks[1:],
        compiler_params=small,
        cost_estimate=pl.CostEstimate(flops=4 << 30, bytes_accessed=12 << 20, transcendentals=0),
        name="add_trials",
    )(places, wide)
    arrived = [rest[-1]]
    for step, sums in zip(steps[:-1], [first] + list(rest[:-1])):
        pairs = [(place, partner(place, step, bands)) for place in range(bands)]
        arrived.append(lax.ppermute(sums, "band", pairs))
    series, peaks = pl.pallas_call(
        functools.partial(peak_kernel, beams, math.sqrt(channels * bands)),
        in_specs=[in_smem] + [in_vmem] * bands,
        out_specs=[in_vmem] * 2,
        out_shape=[
            jax.ShapeDtypeStruct((beams, count, length), jnp.bfloat16),
            jax.ShapeDtypeStruct((beams, widths.shape[0], count), jnp.float32),
        ],
        compiler_params=small,
        name="boxcar_peaks",
    )(widths, *arrived)
    return series, peaks.swapaxes(1, 2)


def solution(mesh):
    return jax.shard_map(
        lambda *arrays: tuple(local(*arrays)),
        mesh=mesh,
        in_specs=(
            P(None, "band", "trial"),
            P("band", None, None),
            P(),
            P("trial", None),
            P("trial", None),
            P(),
        ),
        out_specs=(P(None, ("trial", "band"), None), P(None, ("trial", "band"), None)),
        check_vma=False,
    )
```

time: 54.8 us -> 42.8 us (0.78)
  Pallas kernels: 27.1 us -> 16.8 us
  local copies, waits for them, and re-layouts: 3.45 us -> 0.01 us
  waiting for transfers between devices: 12.2 us -> 14.2 us
  other arithmetic: 1.38 us -> 0.78 us
    pallas_call x5 -> x3, Pallas kernels: 24.8 us -> 15.1 us  [the longest x1 10.4 us: local(): pl.pallas_call(functools.partial(fine_kernel, sources), in_specs=[in_smem...]
    unnamed x8 -> x2, local copies, waits for them, and re-layouts: 2.06 us -> 0.01 us
    ppermute x3, waiting for transfers between devices: 6.27 us -> 7.74 us  [local(): arrived.append(lax.ppermute(sums, 'band', pairs))]
    pallas_call x1 -> x0, local copies, waits for them, and re-layouts: 1.39 us -> none  [local(): pl.pallas_call(functools.partial(peak_kernel, beams, math.sqrt(channels *...]
    add x1, other arithmetic: 1.37 us -> 0.78 us  [local(): places = (pair * QSPAN + own_rel << 20) + own_shift]
    all_to_all x1, waiting for transfers between devices: 5.9 us -> 6.5 us  [local(): lax.all_to_all(send, 'trial', split_axis=0, concat_axis=0, tiled=True)]
  transfers between devices with their start and end apart: 4 -> 4, of which waited for: 2 -> 3; matrix products, arithmetic and copies ran while one was open for 3% -> 2% of each run, Pallas kernels for 6% -> 0%
where the time goes in v2:
time: 42.8 us; the launch traced here: 42.2 us
  Pallas kernels  16.8 us (39%)
  waiting for transfers between devices  14.2 us (33%)
  starting transfers between devices  9.63 us (23%)
  other arithmetic  0.78 us (2%)
  between operations  0.67 us (2%)
    pallas_call x1, Pallas kernels, local(): pl.pallas_call(functools.partial(fine_kernel, sources), in_specs=[in_smem...  10.4 us
    ppermute x3, waiting for transfers between devices, local(): arrived.append(lax.ppermute(sums, 'band', pairs))  7.74 us
    all_to_all x1, waiting for transfers between devices, local(): lax.all_to_all(send, 'trial', split_axis=0, concat_axis=0, tiled=True)  6.5 us
    all_to_all x1, starting transfers between devices, local(): lax.all_to_all(send, 'trial', split_axis=0, concat_axis=0, tiled=True)  5.18 us
    ppermute x3, starting transfers between devices, local(): arrived.append(lax.ppermute(sums, 'band', pairs))  4.45 us
    pallas_call x1, Pallas kernels, local(): pl.pallas_call(functools.partial(next_kernel, subs, beams, bands, steps[1...  3.02 us
    pallas_call x1, Pallas kernels, local(): pl.pallas_call(functools.partial(peak_kernel, beams, math.sqrt(channels *...  1.77 us
    pallas_call x1, Pallas kernels, local(): pl.pallas_call(functools.partial(first_kernel, subs, beams, packed, bands...  1.65 us
  transfers between devices with their start and end apart: 4, of which 3 were waited for; matrix products, arithmetic and copies ran while one was open for 2% of the time, Pallas kernels for 0%

profile of v2, /device:TPU:0, one launch (start us, length us, event | category | flops | bytes accessed | tf_op | source)
XLA Modules:
  0.0 42.2 jit_solution(10307487347915370758)
XLA Ops:
  0.6 10.4 %fine_delays.1 = bf16[8,144,128]{2,1,0:T(8,128)(2,1)} custom-call(s32[8,32]{1,0:T(8,128)} %span_ref.1, bf16[2,4096,256]{2,1,0:T(8,128)(2,1)} %x_hbm.1, s32[8,32,512]{2,1,0:T(8,128)} %delay_ref.1), custom_call_target="tpu_custom_call" | custom-call | tf_op jit(solution)/shard_map/fine_delays/pallas_call | solution.py:234
  11.0 5.2 %all-to-all-start = ((bf16[8,144,128]{2,1,0:T(8,128)(2,1)}), bf16[8,144,128]{2,1,0:T(8,128)(2,1)S(1)}, u32[]{:S(2)}, u32[]{:S(2)}) async-start(bf16[8,144,128]{2,1,0:T(8,128)(2,1)} %fine_delays.1), calls=%async_computation | async-start | bytes 589824 | tf_op jit(solution)/shard_map/all_to_all | solution.py:254
  16.2 0.8 %add_bitcast_fusion.place_ref = s32[8,64]{1,0:T(8,128)S(1)} fusion(s32[64,32]{0,1:T(8,128)} %param.10, s32[]{:T(128)S(6)} %select_n.4, s32[64,32]{0,1:T(8,128)} %param.9, s32[8]{0:T(128)S(1)} %iota_multiply_fusion), kind=kLoop, calls=%fused_computation | loop fusion | flops 1536 | bytes 6180 | tf_op jit(solution)/shard_map/add | solution.py:253
  17.0 6.5 %all-to-all-done.recv_ref = bf16[8,144,128]{2,1,0:T(8,128)(2,1)S(1)} async-done(((bf16[8,144,128]{2,1,0:T(8,128)(2,1)}), bf16[8,144,128]{2,1,0:T(8,128)(2,1)S(1)}, u32[]{:S(2)}, u32[]{:S(2)}) %all-to-all-start) | async-done | bytes 294944 | tf_op jit(solution)/shard_map/all_to_all | solution.py:254
  23.5 1.6 %spread_and_add.1 = (f32[64,32,128]{2,1,0:T(8,128)S(1)}, bf16[16,32,128]{2,1,0:T(8,128)(2,1)S(1)}) custom-call(s32[8,64]{1,0:T(8,128)S(1)} %add_bitcast_fusion.place_ref, bf16[8,144,128]{2,1,0:T(8,128)(2,1)S(1)} %all-to-all-done.recv_ref), custom_call_target="tpu_custom_call" | custom-call | tf_op jit(solution)/shard_map/spread_and_add/pallas_call | solution.py:261
  25.2 0.0 copy-start
  25.2 3.0 %add_trials.1 = (bf16[16,32,128]{2,1,0:T(8,128)(2,1)S(1)}, bf16[16,32,128]{2,1,0:T(8,128)(2,1)S(1)}, f32[16,32,128]{2,1,0:T(8,128)S(1)}) custom-call(s32[8,64]{1,0:T(8,128)S(1)} %add_bitcast_fusion.place_ref, f32[64,32,128]{2,1,0:T(8,128)S(1)} %get-tuple-element.9.wide_ref), custom_call_target="tpu_custom_call" | custom-call | flops 4294967296 | bytes 12582912 | tf_op jit(solution)/shard_map/add_trials/pallas_call | solution.py:270
  28.2 2.7 %collective-permute-start.1 = (bf16[16,32,128]{2,1,0:T(8,128)(2,1)S(1)}, bf16[16,32,128]{2,1,0:T(8,128)(2,1)S(1)}, u32[]{:S(2)}, u32[]{:S(2)}) collective-permute-start(bf16[16,32,128]{2,1,0:T(8,128)(2,1)S(1)} %get-tuple-element.12), channel_id=1, source_target_pairs={{0,16},{8,24},{16,0},{24,8},{1,17},{9,25},{17,1},{25,9},{2,18},{10... | collective-permute-start | bytes 393224 | tf_op jit(solution)/shard_map/ppermute | solution.py:283
  30.9 1.6 %collective-permute-start.2 = (bf16[16,32,128]{2,1,0:T(8,128)(2,1)S(1)}, bf16[16,32,128]{2,1,0:T(8,128)(2,1)S(1)}, u32[]{:S(2)}, u32[]{:S(2)}) collective-permute-start(bf16[16,32,128]{2,1,0:T(8,128)(2,1)S(1)} %get-tuple-element.13), channel_id=1, source_target_pairs={{0,8},{8,0},{16,24},{24,16},{1,9},{9,1},{17,25},{25,17},{2,10},{10... | collective-permute-start | bytes 393224 | tf_op jit(solution)/shard_map/ppermute | solution.py:283
  32.4 0.2 collective-permute-start
  32.6 6.3 %collective-permute-done.1.refs_2_ = bf16[16,32,128]{2,1,0:T(8,128)(2,1)S(1)} collective-permute-done((bf16[16,32,128]{2,1,0:T(8,128)(2,1)S(1)}, bf16[16,32,128]{2,1,0:T(8,128)(2,1)S(1)}, u32[]{:S(2)}, u32[]{:S(2)}) %collective-permute-start.1) | collective-permute-done | bytes 131104 | tf_op jit(solution)/shard_map/ppermute | solution.py:283
  39.0 0.0 collective-permute-done.2.refs_3_
  39.0 1.4 %collective-permute-done.refs_1_ = bf16[16,32,128]{2,1,0:T(8,128)(2,1)S(1)} collective-permute-done((bf16[16,32,128]{2,1,0:T(8,128)(2,1)S(1)}, bf16[16,32,128]{2,1,0:T(8,128)(2,1)S(1)}, u32[]{:S(2)}, u32[]{:S(2)}) %collective-permute-start) | collective-permute-done | bytes 131104 | tf_op jit(solution)/shard_map/ppermute | solution.py:283
  40.4 0.0 copy-done
  40.4 1.8 %boxcar_peaks.1 = (bf16[2,16,2048]{2,1,0:T(8,128)(2,1)}, f32[2,4,16]{2,1,0:T(4,128)}) custom-call(s32[4]{0:T(128)S(1)} %copy-done, f32[16,32,128]{2,1,0:T(8,128)S(1)} %get-tuple-element.10.refs_0_, bf16[16,32,128]{2,1,0:T(8,128)(2,1)S(1)} %collective-permute-done.refs_1_, bf16[16,32,128]{2,1,0:T(8,128)(2,1)S(1)} %collective-permute-done.1.refs_2_, ...), custom_call_target="tpu_custom_call" | custom-call | tf_op jit(solution)/shard_map/boxcar_peaks/pallas_call | solution.py:284
  (1 shorter events, 0.0 us)
Async XLA Ops:
  11.0 12.5 %all-to-all-start = ((bf16[8,144,128]{2,1,0:T(8,128)(2,1)}), bf16[8,144,128]{2,1,0:T(8,128)(2,1)S(1)}, u32[]{:S(2)}, u32[]{:S(2)}) async-start(bf16[8,144,128]{2,1,0:T(8,128)(2,1)} %fine_delays.1), calls=%async_computation | async-start | bytes 589824 | tf_op jit(solution)/shard_map/all_to_all | solution.py:254
  25.2 15.2 %copy-start = (s32[4]{0:T(128)S(1)}, s32[4]{0:T(128)}, u32[]{:S(2)}) copy-start(s32[4]{0:T(128)} %width_ref.1) | copy-start | bytes 52
  28.2 10.8 %collective-permute-start.1 = (bf16[16,32,128]{2,1,0:T(8,128)(2,1)S(1)}, bf16[16,32,128]{2,1,0:T(8,128)(2,1)S(1)}, u32[]{:S(2)}, u32[]{:S(2)}) collective-permute-start(bf16[16,32,128]{2,1,0:T(8,128)(2,1)S(1)} %get-tuple-element.12), channel_id=1, source_target_pairs={{0,16},{8,24},{16,0},{24,8},{1,17},{9,25},{17,1},{25,9},{2,18},{10... | collective-permute-start | bytes 393224 | tf_op jit(solution)/shard_map/ppermute | solution.py:283
  30.9 8.1 %collective-permute-start.2 = (bf16[16,32,128]{2,1,0:T(8,128)(2,1)S(1)}, bf16[16,32,128]{2,1,0:T(8,128)(2,1)S(1)}, u32[]{:S(2)}, u32[]{:S(2)}) collective-permute-start(bf16[16,32,128]{2,1,0:T(8,128)(2,1)S(1)} %get-tuple-element.13), channel_id=1, source_target_pairs={{0,8},{8,0},{16,24},{24,16},{1,9},{9,1},{17,25},{25,17},{2,10},{10... | collective-permute-start | bytes 393224 | tf_op jit(solution)/shard_map/ppermute | solution.py:283
  32.4 8.0 %collective-permute-start = (bf16[16,32,128]{2,1,0:T(8,128)(2,1)S(1)}, bf16[16,32,128]{2,1,0:T(8,128)(2,1)S(1)}, u32[]{:S(2)}, u32[]{:S(2)}) collective-permute-start(bf16[16,32,128]{2,1,0:T(8,128)(2,1)S(1)} %get-tuple-element.11), channel_id=1, source_target_pairs={{0,24},{8,16},{16,8},{24,0},{1,25},{9,17},{17,9},{25,1},{2,26},{10... | collective-permute-start | bytes 393224 | tf_op jit(solution)/shard_map/ppermute | solution.py:283

commit v3 on v2

--- a/solution.py
+++ b/solution.py
@@ -17,49 +17,95 @@
     return (number + step - 1) // step * step
 
 
-def fine_kernel(trial_ranges, span_ref, x_hbm, delay_ref, out_ref, x_ref, lagged_ref, joined_ref, tail_ref, sems):
+def fine_kernel(trial_ranges, span_ref, x_hbm, delay_hbm, *refs):
+    (keep_ref, swap_ref, x_ref, delay_ref, turned_ref, lagged_ref, joined_ref, tail_ref, sems) = refs
     subs, beams, width, block_len = x_ref.shape
     q_count = delay_ref.shape[1]
     packed = LANES // q_count
-    tiles = MAXD1 // packed
+    step = MAXD1 // 2
+    tiles = step // packed
     halves = block_len // LANES
     reach = MAXD1 + block_len
     unit = trial_ranges * QSPAN * packed
     per_range = QSPAN * packed
+    lead = min(3, subs)
+    early = 1
     copies = [
         pltpu.make_async_copy(x_hbm.at[:, pl.ds(sub * width, width), :], x_ref.at[sub], sems.at[sub])
         for sub in range(subs)
     ]
-    for copy in copies:
-        copy.start()
-    for beam in range(beams):
-        lagged_ref[beam, :MAXD1, :] = jnp.zeros((MAXD1, MAXD1 * q_count), jnp.float32)
-        lagged_ref[beam, reach:, :] = jnp.zeros((MAXD1, MAXD1 * q_count), jnp.float32)
-    joined_ref[:, :, reach:, :] = jnp.zeros((packed, beams, 8, LANES), jnp.float32)
+    delay_copies = [
+        pltpu.make_async_copy(delay_hbm.at[pl.ds(0, early)], delay_ref.at[pl.ds(0, early)], sems.at[subs]),
+        pltpu.make_async_copy(delay_hbm.at[pl.ds(early, subs - early)], delay_ref.at[pl.ds(early, subs - early)], sems.at[subs + 1]),
+    ]
+    delay_copies[0].start()
+    copies[0].start()
+    copies[1].start()
+    delay_copies[1].start()
+    for sub in range(2, lead):
+        copies[sub].start()
+    for parity in range(turned_ref.shape[0]):
+        for beam in range(beams):
+            turned_ref[parity, beam, :step, :] = jnp.zeros((step, width), jnp.bfloat16)
+            turned_ref[parity, beam, step + block_len :, :] = jnp.zeros((step, width), jnp.bfloat16)
+    for parity in range(lagged_ref.shape[0]):
+        for beam in range(beams):
+            lagged_ref[parity, beam, :step, :] = jnp.zeros((step, step * q_count), jnp.float32)
+            lagged_ref[parity, beam, reach:, :] = jnp.zeros((step, step * q_count), jnp.float32)
+    joined_ref[:, :, reach:, :] = jnp.zeros((subs, beams, 8, LANES), jnp.float32)
+    lane_part = (lax.broadcasted_iota(jnp.int32, (width, LANES), 1) // q_count).astype(jnp.float32)
     own = lax.axis_index("band") * subs
+    me = lax.axis_index("trial")
     lane = lax.broadcasted_iota(jnp.int32, (8, LANES), 1)
     row_id = lax.broadcasted_iota(jnp.int32, (QSPAN * packed, LANES), 0)
     lane_id = lax.broadcasted_iota(jnp.int32, (QSPAN * packed, LANES), 1)
     tail_row = lax.broadcasted_iota(jnp.int32, (trial_ranges * packed, LANES), 0)
     tail_lane = lax.broadcasted_iota(jnp.int32, (trial_ranges * packed, LANES), 1)
-    for group in range(subs // packed):
-        for place in range(packed):
-            sub = group * packed + place
-            tiled = jnp.concatenate([delay_ref[sub]] * packed, axis=0).astype(jnp.float32).T
-            tiled = tiled - (lax.broadcasted_iota(jnp.int32, tiled.shape, 1) // q_count).astype(jnp.float32)
-            selector = jnp.concatenate([jnp.where(tiled == jnp.float32(tile * packed), 1.0, 0.0).astype(jnp.bfloat16) for tile in range(tiles)], axis=1)
-            copies[sub].wait()
-            for beam in range(beams):
-                lagged_ref[beam, MAXD1:reach, :] = lax.dot_general(
-                    x_ref[sub, beam], selector, (((0,), (0,)), ((), ())), preferred_element_type=jnp.float32
+    def one_sub(sub):
+        if sub == 0:
+            delay_copies[0].wait()
+        if sub == early:
+            delay_copies[1].wait()
+        tiled = jnp.concatenate([delay_ref[sub]] * packed, axis=0).astype(jnp.float32).T - lane_part
+        selector = jnp.concatenate(
+            [
+                jnp.concatenate(
+                    [
+                        jnp.where(tiled == jnp.float32(half * step + tile * packed), 1.0, 0.0).astype(jnp.bfloat16)
+                        for tile in range(tiles)
+                    ],
+                    axis=1,
                 )
-                for start in range(0, reach, 8):
-                    total = lagged_ref[beam, start : start + 8, :LANES]
-                    for tile in range(1, tiles):
-                        at = start + packed * tile
-                        total = total + lagged_ref[beam, at : at + 8, tile * LANES : (tile + 1) * LANES]
-                    joined_ref[place, beam, start : start + 8, :] = total
-        firsts = [[span_ref[target, own + group * packed + place] for place in range(packed)] for target in range(trial_ranges)]
+                for half in range(2)
+            ],
+            axis=0,
+        )
+        copies[sub].wait()
+        if sub + lead < subs:
+            copies[sub + lead].start()
+        side, other = sub % turned_ref.shape[0], sub % lagged_ref.shape[0]
+        left = []
+        for beam in range(beams):
+            turned_ref[side, beam, step : step + block_len, :] = x_ref[sub, beam].T
+            left.append(
+                jnp.concatenate(
+                    [turned_ref[side, beam, : step + block_len, :], turned_ref[side, beam, step : 2 * step + block_len, :]],
+                    axis=1,
+                )
+            )
+        both = jnp.dot(jnp.concatenate(left, axis=0), selector, preferred_element_type=jnp.float32)
+        for beam in range(beams):
+            lagged_ref[other, beam, step:reach, :] = both[beam * (step + block_len) : (beam + 1) * (step + block_len)]
+        for beam in range(beams):
+            for start in range(0, reach, 8):
+                total = lagged_ref[other, beam, start : start + 8, :LANES]
+                for tile in range(1, tiles):
+                    at = start + packed * tile
+                    total = total + lagged_ref[other, beam, at : at + 8, tile * LANES : (tile + 1) * LANES]
+                joined_ref[sub, beam, start : start + 8, :] = total
+
+    def choose(group):
+        firsts = [[span_ref[me ^ target, own + group * packed + place] for place in range(packed)] for target in range(trial_ranges)]
         chooser = []
         for target in range(trial_ranges):
             column = jnp.zeros((per_range, LANES), jnp.int32)
@@ -80,7 +126,7 @@
                     mixed = None
                     for part in range(packed):
                         there = (part + turn) % packed
-                        piece = joined_ref[there, beam, start + part : start + part + 8, :]
+                        piece = joined_ref[group * packed + there, beam, start + part : start + part + 8, :]
                         mixed = piece if mixed is None else jnp.where(lane >= part * q_count, piece, mixed)
                     if turn:
                         mixed = pltpu.roll(mixed, turn * q_count, 1)
@@ -93,28 +139,43 @@
             for target in range(trial_ranges):
                 for half in range(halves):
                     at = ((group * beams + beam) * halves + half) * per_range
-                    out_ref[target, at : at + per_range, :] = chosen[
+                    (keep_ref, swap_ref)[target % 2][target // 2, at : at + per_range, :] = chosen[
                         target * per_range : (target + 1) * per_range, half * LANES : (half + 1) * LANES
                     ]
             tails = lax.dot_general(
                 tail_chooser, rows[block_len:], (((1,), (1,)), ((), ())), preferred_element_type=jnp.float32
             )
-            step = trial_ranges * packed
-            tails = jnp.concatenate([tails[span * step : (span + 1) * step] for span in range(QSPAN)], axis=1)
+            units = trial_ranges * packed
+            tails = jnp.concatenate([tails[span * units : (span + 1) * units] for span in range(QSPAN)], axis=1)
             for target in range(trial_ranges):
                 tail_ref[target, pl.ds((group * beams + beam) * packed, packed), :] = tails[target * packed : (target + 1) * packed]
+
+    for sub in range(subs):
+        one_sub(sub)
+        if sub and sub % packed == 0:
+            choose(sub // packed - 1)
+    choose(subs // packed - 1)
     main = subs * beams * halves * QSPAN
     for target in range(trial_ranges):
-        out_ref[target, main:, :] = tail_ref[target].astype(jnp.bfloat16)
-
-
-def spread(subs, beams, packed, recv_ref, wide_ref, flat_ref):
-    sources, rows, _ = recv_ref.shape
+        (keep_ref, swap_ref)[target % 2][target // 2, main:, :] = tail_ref[target].astype(jnp.bfloat16)
+
+
+def pair_kernel(keep_ref, swap_ref, *out_refs):
+    for place, out_ref in enumerate(out_refs):
+        out_ref[0] = keep_ref[place]
+        out_ref[1] = swap_ref[place]
+
+
+def spread(subs, beams, packed, recv_refs, wide_ref, flat_ref):
+    _, rows, _ = recv_refs[0].shape
+    sources = 2 * len(recv_refs)
     halves = 2
     blocks = sources * halves
     main = subs * beams * halves * QSPAN
-    for source in range(sources):
-        flat_ref[source * rows : (source + 1) * rows] = recv_ref[source].astype(jnp.float32)
+    me = lax.axis_index("trial")
+    for step in range(sources):
+        at = pl.multiple_of((me ^ step) * rows, 16)
+        flat_ref[pl.ds(at, rows), :] = recv_refs[step // 2][step % 2].astype(jnp.float32)
     flat_ref[sources * rows :] = jnp.zeros((rows, LANES), jnp.float32)
     lane = lax.broadcasted_iota(jnp.int32, (sources, LANES), 1)
     for pair in range(subs * beams):
@@ -170,8 +231,9 @@
     return place ^ step if peers & (peers - 1) == 0 else (place + step) % peers
 
 
-def first_kernel(subs, beams, packed, bands, step, count, place_ref, recv_ref, wide_ref, out_ref, flat_ref, sums_ref):
-    spread(subs, beams, packed, recv_ref, wide_ref, flat_ref)
+def first_kernel(subs, beams, packed, bands, step, count, place_ref, *refs):
+    wide_ref, out_ref, flat_ref, sums_ref = refs[-4:]
+    spread(subs, beams, packed, refs[:-4], wide_ref, flat_ref)
     band = partner(lax.axis_index("band"), step, bands)
     add_trials(subs, beams, band * count, count, place_ref, wide_ref, sums_ref, out_ref)
 
@@ -231,18 +293,21 @@
     in_smem = pl.BlockSpec(memory_space=pltpu.SMEM)
     in_vmem = pl.BlockSpec(memory_space=pltpu.VMEM)
     small = pltpu.CompilerParams(vmem_limit_bytes=16 << 20)
-    send = pl.pallas_call(
+    chips = sources // 2
+    keep, swap = pl.pallas_call(
         functools.partial(fine_kernel, sources),
-        in_specs=[in_smem, pl.BlockSpec(memory_space=pl.ANY), in_vmem],
-        out_specs=in_vmem,
+        in_specs=[in_smem] + [pl.BlockSpec(memory_space=pl.ANY)] * 2,
+        out_specs=[in_vmem] * 2,
         scratch_shapes=[
             pltpu.VMEM((subs, beams, width, block_len), jnp.bfloat16),
-            pltpu.VMEM((beams, block_len + 2 * MAXD1, MAXD1 * q_count), jnp.float32),
-            pltpu.VMEM((packed, beams, block_len + MAXD1 + 8, LANES), jnp.float32),
+            pltpu.VMEM((subs, q_count, width), jnp.int32),
+            pltpu.VMEM((1, beams, block_len + MAXD1, width), jnp.bfloat16),
+            pltpu.VMEM((1, beams, block_len + MAXD1 + MAXD1 // 2, MAXD1 // 2 * q_count), jnp.float32),
+            pltpu.VMEM((subs, beams, block_len + MAXD1 + 8, LANES), jnp.float32),
             pltpu.VMEM((sources, rows - main, LANES), jnp.float32),
-            pltpu.SemaphoreType.DMA((subs,)),
+            pltpu.SemaphoreType.DMA((subs + 2,)),
         ],
-        out_shape=jax.ShapeDtypeStruct((sources, rows, LANES), jnp.bfloat16),
+        out_shape=[pltpu.VMEM((chips, rows, LANES), jnp.bfloat16)] * 2,
         compiler_params=pltpu.CompilerParams(vmem_limit_bytes=61 << 20),
         name="fine_delays",
     )(span_start, intensity, fine_delay)
@@ -251,7 +316,19 @@
     own_shift = lax.dynamic_slice_in_dim(offset.T, own, subs, 0)
     pair = jnp.arange(subs, dtype=jnp.int32)[:, None] * beams
     places = ((pair * QSPAN + own_rel) << 20) + own_shift
-    received = lax.all_to_all(send, "trial", split_axis=0, concat_axis=0, tiled=True)
+
+    def crossed(array, step):
+        return lax.ppermute(array, "trial", [(place, place ^ step) for place in range(sources)])
+
+    pairs = pl.pallas_call(
+        pair_kernel,
+        in_specs=[in_vmem] * 2,
+        out_specs=[in_vmem] * chips,
+        out_shape=[jax.ShapeDtypeStruct((2, rows, LANES), jnp.bfloat16)] * chips,
+        compiler_params=small,
+        name="pair_rows",
+    )(keep, crossed(swap, 1))
+    received = [pairs[0]] + [crossed(pairs[step], 2 * step) for step in range(1, chips)]
     stride = round_up(blocks + length // 2 // LANES + 1, 8)
     count = trials // bands
     chunk_shape = (blocks, beams * count, LANES)
@@ -260,13 +337,13 @@
     chunks = [jax.ShapeDtypeStruct(chunk_shape, jnp.bfloat16 if step else jnp.float32) for step in steps]
     wide, first = pl.pallas_call(
         functools.partial(first_kernel, subs, beams, packed, bands, steps[0], count),
-        in_specs=[in_smem, in_vmem],
+        in_specs=[in_smem] + [in_vmem] * chips,
         out_specs=[in_vmem, in_vmem],
         scratch_shapes=[pltpu.VMEM(((sources + 1) * rows, LANES), jnp.float32), sums_scratch],
         out_shape=[jax.ShapeDtypeStruct((subs * beams * QSPAN, stride, LANES), jnp.float32), chunks[0]],
         compiler_params=small,
         name="spread_and_add",
-    )(places, received)
+    )(places, *received)
     rest = pl.pallas_call(
         functools.partial(next_kernel, subs, beams, bands, steps[1:], count),
         in_specs=[in_smem, in_vmem],
@@ -277,13 +354,14 @@
         cost_estimate=pl.CostEstimate(flops=4 << 30, bytes_accessed=12 << 20, transcendentals=0),
         name="add_trials",
     )(places, wide)
-    arrived = [rest[-1]]
+    arrived = []
     for step, sums in zip(steps[:-1], [first] + list(rest[:-1])):
         pairs = [(place, partner(place, step, bands)) for place in range(bands)]
         arrived.append(lax.ppermute(sums, "band", pairs))
+    arrived = [rest[-1] + arrived[0].astype(jnp.float32)] + arrived[1:]
     series, peaks = pl.pallas_call(
         functools.partial(peak_kernel, beams, math.sqrt(channels * bands)),
-        in_specs=[in_smem] + [in_vmem] * bands,
+        in_specs=[in_smem] + [in_vmem] * len(arrived),
         out_specs=[in_vmem] * 2,
         out_shape=[
             jax.ShapeDtypeStruct((beams, count, length), jnp.bfloat16),

time: 42.8 us -> 38.3 us (0.89); the launches traced: 42.2 us -> 38.1 us
  waiting for transfers between devices: 14.2 us -> 11.4 us
  Pallas kernels: 16.8 us -> 15.8 us
    all_to_all x1 -> x0, waiting for transfers between devices: 6.5 us -> none  [local(): lax.all_to_all(send, 'trial', split_axis=0, concat_axis=0, tiled=True)]
    ppermute x0 -> x4, waiting for transfers between devices: none -> 5.46 us  [crossed(): lax.ppermute(array, 'trial', [(place, place ^ step) for place in range(so...]
    all_to_all x1 -> x0, starting transfers between devices: 5.18 us -> none  [local(): lax.all_to_all(send, 'trial', split_axis=0, concat_axis=0, tiled=True)]
    ppermute x0 -> x4, starting transfers between devices: none -> 4.97 us  [crossed(): lax.ppermute(array, 'trial', [(place, place ^ step) for place in range(so...]
    ppermute x3, waiting for transfers between devices: 7.74 us -> 5.92 us  [local(): arrived.append(lax.ppermute(sums, 'band', pairs))]
    pallas_call x1, Pallas kernels: 10.4 us -> 9.27 us  [local(): pl.pallas_call(functools.partial(fine_kernel, sources), in_specs=[in_smem...]
  transfers between devices with their start and end apart: 4 -> 7, of which waited for: 3 -> 5; matrix products, arithmetic and copies ran while one was open for 2% -> 2% of each run, Pallas kernels for 0% -> 8%
where the time goes in v3:
time: 38.3 us; the launch traced here: 38.1 us
  Pallas kernels  15.8 us (41%)
  waiting for transfers between devices  11.4 us (30%)
  starting transfers between devices  9.48 us (25%)
  other arithmetic  0.81 us (2%)
  between operations  0.68 us (2%)
    pallas_call x1, Pallas kernels, local(): pl.pallas_call(functools.partial(fine_kernel, sources), in_specs=[in_smem...  9.27 us
    ppermute x3, waiting for transfers between devices, local(): arrived.append(lax.ppermute(sums, 'band', pairs))  5.92 us
    ppermute x4, waiting for transfers between devices, crossed(): lax.ppermute(array, 'trial', [(place, place ^ step) for place in range(so...  5.46 us
    ppermute x4, starting transfers between devices, crossed(): lax.ppermute(array, 'trial', [(place, place ^ step) for place in range(so...  4.97 us
    ppermute x3, starting transfers between devices, local(): arrived.append(lax.ppermute(sums, 'band', pairs))  4.51 us
    pallas_call x1, Pallas kernels, local(): pl.pallas_call(functools.partial(next_kernel, subs, beams, bands, steps[1...  3.01 us
    pallas_call x1, Pallas kernels, local(): pl.pallas_call(functools.partial(peak_kernel, beams, math.sqrt(channels *...  1.76 us
    pallas_call x1, Pallas kernels, local(): pl.pallas_call(functools.partial(first_kernel, subs, beams, packed, bands...  1.68 us
  transfers between devices with their start and end apart: 7, of which 5 were waited for; matrix products, arithmetic and copies ran while one was open for 2% of the time, Pallas kernels for 8%

profile of v3, /device:TPU:0, one launch (start us, length us, event | category | flops | bytes accessed | tf_op | source)
XLA Modules:
  0.0 38.1 jit_solution(16635012665652295453)
XLA Ops:
  0.6 9.3 %fine_delays.1 = (bf16[4,144,128]{2,1,0:T(8,128)(2,1)S(1)}, bf16[4,144,128]{2,1,0:T(8,128)(2,1)S(1)}) custom-call(s32[8,32]{1,0:T(8,128)} %span_ref.1, bf16[2,4096,256]{2,1,0:T(8,128)(2,1)} %x_hbm.1, s32[8,32,512]{2,1,0:T(8,128)} %delay_hbm.1), custom_call_target="tpu_custom_call" | custom-call | tf_op jit(solution)/shard_map/fine_delays/pallas_call | solution.py:297
  9.9 0.5 %collective-permute-start = (bf16[4,144,128]{2,1,0:T(8,128)(2,1)S(1)}, bf16[4,144,128]{2,1,0:T(8,128)(2,1)S(1)}, u32[]{:S(2)}, u32[]{:S(2)}) collective-permute-start(bf16[4,144,128]{2,1,0:T(8,128)(2,1)S(1)} %get-tuple-element.16), channel_id=1, source_target_pairs={{0,1},{1,0},{2,3},{3,2},{4,5},{5,4},{6,7},{7,6},{8,9},{9,8},{10,11... | collective-permute-start | bytes 442376 | tf_op jit(solution)/shard_map/ppermute | solution.py:321
  10.4 1.0 %collective-permute-done.swap_ref = bf16[4,144,128]{2,1,0:T(8,128)(2,1)S(1)} collective-permute-done((bf16[4,144,128]{2,1,0:T(8,128)(2,1)S(1)}, bf16[4,144,128]{2,1,0:T(8,128)(2,1)S(1)}, u32[]{:S(2)}, u32[]{:S(2)}) %collective-permute-start) | collective-permute-done | bytes 147488 | tf_op jit(solution)/shard_map/ppermute | solution.py:321
  11.5 2.9 %collective-permute-start.1 = (bf16[2,144,128]{2,1,0:T(8,128)(2,1)S(1)}, bf16[2,144,128]{2,1,0:T(8,128)(2,1)S(1)}, u32[]{:S(2)}, u32[]{:S(2)}) collective-permute-start(bf16[2,144,128]{2,1,0:T(8,128)(2,1)S(1)} %get-tuple-element.18), channel_id=1, source_target_pairs={{0,2},{1,3},{2,0},{3,1},{4,6},{5,7},{6,4},{7,5},{8,10},{9,11},{10,... | collective-permute-start | bytes 221192 | tf_op jit(solution)/shard_map/ppermute | solution.py:321
  14.4 1.5 %collective-permute-start.2 = (bf16[2,144,128]{2,1,0:T(8,128)(2,1)S(1)}, bf16[2,144,128]{2,1,0:T(8,128)(2,1)S(1)}, u32[]{:S(2)}, u32[]{:S(2)}) collective-permute-start(bf16[2,144,128]{2,1,0:T(8,128)(2,1)S(1)} %get-tuple-element.19), channel_id=1, source_target_pairs={{0,4},{1,5},{2,6},{3,7},{4,0},{5,1},{6,2},{7,3},{8,12},{9,13},{10,... | collective-permute-start | bytes 221192 | tf_op jit(solution)/shard_map/ppermute | solution.py:321
  15.9 0.0 collective-permute-start.3
  15.9 0.8 %add_bitcast_fusion.place_ref = s32[8,64]{1,0:T(8,128)S(1)} fusion(s32[64,32]{0,1:T(8,128)} %param.10, s32[]{:T(128)S(6)} %select_n.4, s32[64,32]{0,1:T(8,128)} %param.9, s32[8]{0:T(128)S(1)} %iota_multiply_fusion), kind=kLoop, calls=%fused_computation.1 | loop fusion | flops 1536 | bytes 6180 | tf_op jit(solution)/shard_map/add | solution.py:318
  16.7 0.3 collective-permute-done.1.refs_1_
  17.0 1.8 %collective-permute-done.2.refs_2_ = bf16[2,144,128]{2,1,0:T(8,128)(2,1)S(1)} collective-permute-done((bf16[2,144,128]{2,1,0:T(8,128)(2,1)S(1)}, bf16[2,144,128]{2,1,0:T(8,128)(2,1)S(1)}, u32[]{:S(2)}, u32[]{:S(2)}) %collective-permute-start.2) | collective-permute-done | bytes 73760 | tf_op jit(solution)/shard_map/ppermute | solution.py:321
  18.7 2.4 %collective-permute-done.3.refs_3_ = bf16[2,144,128]{2,1,0:T(8,128)(2,1)S(1)} collective-permute-done((bf16[2,144,128]{2,1,0:T(8,128)(2,1)S(1)}, bf16[2,144,128]{2,1,0:T(8,128)(2,1)S(1)}, u32[]{:S(2)}, u32[]{:S(2)}) %collective-permute-start.3) | collective-permute-done | bytes 73760 | tf_op jit(solution)/shard_map/ppermute | solution.py:321
  21.1 1.7 %spread_and_add.1 = (f32[64,32,128]{2,1,0:T(8,128)S(1)}, bf16[16,32,128]{2,1,0:T(8,128)(2,1)S(1)}) custom-call(s32[8,64]{1,0:T(8,128)S(1)} %add_bitcast_fusion.place_ref, bf16[2,144,128]{2,1,0:T(8,128)(2,1)S(1)} %get-tuple-element.17.refs_0_, bf16[2,144,128]{2,1,0:T(8,128)(2,1)S(1)} %collective-permute-done.1.refs_1_, ...), custom_call_target="tpu_custom_call" | custom-call | tf_op jit(solution)/shard_map/spread_and_add/pallas_call | solution.py:338
  22.8 3.6 %collective-permute-start.4 = (bf16[16,32,128]{2,1,0:T(8,128)(2,1)S(1)}, bf16[16,32,128]{2,1,0:T(8,128)(2,1)S(1)}, u32[]{:S(2)}, u32[]{:S(2)}) collective-permute-start(bf16[16,32,128]{2,1,0:T(8,128)(2,1)S(1)} %get-tuple-element.23), channel_id=1, source_target_pairs={{0,24},{8,16},{16,8},{24,0},{1,25},{9,17},{17,9},{25,1},{2,26},{10... | collective-permute-start | bytes 393224 | tf_op jit(solution)/shard_map/ppermute | solution.py:360
  26.5 0.0 copy-start
  26.5 3.0 %add_trials.1 = (bf16[16,32,128]{2,1,0:T(8,128)(2,1)S(1)}, bf16[16,32,128]{2,1,0:T(8,128)(2,1)S(1)}, f32[16,32,128]{2,1,0:T(8,128)S(1)}) custom-call(s32[8,64]{1,0:T(8,128)S(1)} %add_bitcast_fusion.place_ref, f32[64,32,128]{2,1,0:T(8,128)S(1)} %get-tuple-element.21.wide_ref), custom_call_target="tpu_custom_call" | custom-call | flops 4294967296 | bytes 12582912 | tf_op jit(solution)/shard_map/add_trials/pallas_call | solution.py:347
  29.5 0.1 collective-permute-start.5
  29.6 0.8 %collective-permute-start.6 = (bf16[16,32,128]{2,1,0:T(8,128)(2,1)S(1)}, bf16[16,32,128]{2,1,0:T(8,128)(2,1)S(1)}, u32[]{:S(2)}, u32[]{:S(2)}) collective-permute-start(bf16[16,32,128]{2,1,0:T(8,128)(2,1)S(1)} %get-tuple-element.25), channel_id=1, source_target_pairs={{0,8},{8,0},{16,24},{24,16},{1,9},{9,1},{17,25},{25,17},{2,10},{10... | collective-permute-start | bytes 393224 | tf_op jit(solution)/shard_map/ppermute | solution.py:360
  30.4 0.0 collective-permute-done.4
  30.4 5.9 %collective-permute-done.5.refs_1_ = bf16[16,32,128]{2,1,0:T(8,128)(2,1)S(1)} collective-permute-done((bf16[16,32,128]{2,1,0:T(8,128)(2,1)S(1)}, bf16[16,32,128]{2,1,0:T(8,128)(2,1)S(1)}, u32[]{:S(2)}, u32[]{:S(2)}) %collective-permute-start.5) | collective-permute-done | bytes 131104 | tf_op jit(solution)/shard_map/ppermute | solution.py:360
  36.3 0.0 collective-permute-done.6.refs_2_
  36.3 0.0 copy-done
  36.3 1.8 %boxcar_peaks.1 = (bf16[2,16,2048]{2,1,0:T(8,128)(2,1)}, f32[2,4,16]{2,1,0:T(4,128)}) custom-call(s32[4]{0:T(128)S(1)} %copy-done, f32[16,32,128]{2,1,0:T(8,128)S(1)} %convert_add_fusion.refs_0_, bf16[16,32,128]{2,1,0:T(8,128)(2,1)S(1)} %collective-permute-done.5.refs_1_, bf16[16,32,128]{2,1,0:T(8,128)(2,1)S(1)} %collective-permute-done.6.refs_2_), custom_call_target="tpu_custom_call" | custom-call | tf_op jit(solution)/shard_map/boxcar_peaks/pallas_call | solution.py:362
  (3 shorter events, 0.1 us)
Async XLA Ops:
  9.9 1.5 %collective-permute-start = (bf16[4,144,128]{2,1,0:T(8,128)(2,1)S(1)}, bf16[4,144,128]{2,1,0:T(8,128)(2,1)S(1)}, u32[]{:S(2)}, u32[]{:S(2)}) collective-permute-start(bf16[4,144,128]{2,1,0:T(8,128)(2,1)S(1)} %get-tuple-element.16), channel_id=1, source_target_pairs={{0,1},{1,0},{2,3},{3,2},{4,5},{5,4},{6,7},{7,6},{8,9},{9,8},{10,11... | collective-permute-start | bytes 442376 | tf_op jit(solution)/shard_map/ppermute | solution.py:321
  11.5 5.5 %collective-permute-start.1 = (bf16[2,144,128]{2,1,0:T(8,128)(2,1)S(1)}, bf16[2,144,128]{2,1,0:T(8,128)(2,1)S(1)}, u32[]{:S(2)}, u32[]{:S(2)}) collective-permute-start(bf16[2,144,128]{2,1,0:T(8,128)(2,1)S(1)} %get-tuple-element.18), channel_id=1, source_target_pairs={{0,2},{1,3},{2,0},{3,1},{4,6},{5,7},{6,4},{7,5},{8,10},{9,11},{10,... | collective-permute-start | bytes 221192 | tf_op jit(solution)/shard_map/ppermute | solution.py:321
  14.4 4.4 %collective-permute-start.2 = (bf16[2,144,128]{2,1,0:T(8,128)(2,1)S(1)}, bf16[2,144,128]{2,1,0:T(8,128)(2,1)S(1)}, u32[]{:S(2)}, u32[]{:S(2)}) collective-permute-start(bf16[2,144,128]{2,1,0:T(8,128)(2,1)S(1)} %get-tuple-element.19), channel_id=1, source_target_pairs={{0,4},{1,5},{2,6},{3,7},{4,0},{5,1},{6,2},{7,3},{8,12},{9,13},{10,... | collective-permute-start | bytes 221192 | tf_op jit(solution)/shard_map/ppermute | solution.py:321
  15.9 5.3 %collective-permute-start.3 = (bf16[2,144,128]{2,1,0:T(8,128)(2,1)S(1)}, bf16[2,144,128]{2,1,0:T(8,128)(2,1)S(1)}, u32[]{:S(2)}, u32[]{:S(2)}) collective-permute-start(bf16[2,144,128]{2,1,0:T(8,128)(2,1)S(1)} %get-tuple-element.20), channel_id=1, source_target_pairs={{0,6},{1,7},{2,4},{3,5},{4,2},{5,3},{6,0},{7,1},{8,14},{9,15},{10,... | collective-permute-start | bytes 221192 | tf_op jit(solution)/shard_map/ppermute | solution.py:321
  22.8 7.5 %collective-permute-start.4 = (bf16[16,32,128]{2,1,0:T(8,128)(2,1)S(1)}, bf16[16,32,128]{2,1,0:T(8,128)(2,1)S(1)}, u32[]{:S(2)}, u32[]{:S(2)}) collective-permute-start(bf16[16,32,128]{2,1,0:T(8,128)(2,1)S(1)} %get-tuple-element.23), channel_id=1, source_target_pairs={{0,24},{8,16},{16,8},{24,0},{1,25},{9,17},{17,9},{25,1},{2,26},{10... | collective-permute-start | bytes 393224 | tf_op jit(solution)/shard_map/ppermute | solution.py:360
  26.5 9.8 %copy-start = (s32[4]{0:T(128)S(1)}, s32[4]{0:T(128)}, u32[]{:S(2)}) copy-start(s32[4]{0:T(128)} %width_ref.1) | copy-start | bytes 52
  29.5 6.8 %collective-permute-start.5 = (bf16[16,32,128]{2,1,0:T(8,128)(2,1)S(1)}, bf16[16,32,128]{2,1,0:T(8,128)(2,1)S(1)}, u32[]{:S(2)}, u32[]{:S(2)}) collective-permute-start(bf16[16,32,128]{2,1,0:T(8,128)(2,1)S(1)} %get-tuple-element.24), channel_id=1, source_target_pairs={{0,16},{8,24},{16,0},{24,8},{1,17},{9,25},{17,1},{25,9},{2,18},{10... | collective-permute-start | bytes 393224 | tf_op jit(solution)/shard_map/ppermute | solution.py:360
  29.6 6.7 %collective-permute-start.6 = (bf16[16,32,128]{2,1,0:T(8,128)(2,1)S(1)}, bf16[16,32,128]{2,1,0:T(8,128)(2,1)S(1)}, u32[]{:S(2)}, u32[]{:S(2)}) collective-permute-start(bf16[16,32,128]{2,1,0:T(8,128)(2,1)S(1)} %get-tuple-element.25), channel_id=1, source_target_pairs={{0,8},{8,0},{16,24},{24,16},{1,9},{9,1},{17,25},{25,17},{2,10},{10... | collective-permute-start | bytes 393224 | tf_op jit(solution)/shard_map/ppermute | solution.py:360

commit v4 on v3

--- a/solution.py
+++ b/solution.py
@@ -17,8 +17,8 @@
     return (number + step - 1) // step * step
 
 
-def fine_kernel(trial_ranges, span_ref, x_hbm, delay_hbm, *refs):
-    (keep_ref, swap_ref, x_ref, delay_ref, turned_ref, lagged_ref, joined_ref, tail_ref, sems) = refs
+def fine_kernel(trial_ranges, span_any, x_hbm, delay_hbm, *refs):
+    (keep_ref, swap_ref, x_ref, delay_ref, turned_ref, lagged_ref, joined_ref, tail_ref, span_ref, sems) = refs
     subs, beams, width, block_len = x_ref.shape
     q_count = delay_ref.shape[1]
     packed = LANES // q_count
@@ -38,8 +38,10 @@
         pltpu.make_async_copy(delay_hbm.at[pl.ds(0, early)], delay_ref.at[pl.ds(0, early)], sems.at[subs]),
         pltpu.make_async_copy(delay_hbm.at[pl.ds(early, subs - early)], delay_ref.at[pl.ds(early, subs - early)], sems.at[subs + 1]),
     ]
+    span_copy = pltpu.make_async_copy(span_any, span_ref, sems.at[subs + 2])
     delay_copies[0].start()
     copies[0].start()
+    span_copy.start()
     copies[1].start()
     delay_copies[1].start()
     for sub in range(2, lead):
@@ -105,6 +107,8 @@
                 joined_ref[sub, beam, start : start + 8, :] = total
 
     def choose(group):
+        if group == 0:
+            span_copy.wait()
         firsts = [[span_ref[me ^ target, own + group * packed + place] for place in range(packed)] for target in range(trial_ranges)]
         chooser = []
         for target in range(trial_ranges):
@@ -175,7 +179,7 @@
     me = lax.axis_index("trial")
     for step in range(sources):
         at = pl.multiple_of((me ^ step) * rows, 16)
-        flat_ref[pl.ds(at, rows), :] = recv_refs[step // 2][step % 2].astype(jnp.float32)
+        flat_ref[pl.ds(at, rows), :] = recv_refs[-1 - step // 2][step % 2].astype(jnp.float32)
     flat_ref[sources * rows :] = jnp.zeros((rows, LANES), jnp.float32)
     lane = lax.broadcasted_iota(jnp.int32, (sources, LANES), 1)
     for pair in range(subs * beams):
@@ -231,9 +235,12 @@
     return place ^ step if peers & (peers - 1) == 0 else (place + step) % peers
 
 
-def first_kernel(subs, beams, packed, bands, step, count, place_ref, *refs):
-    wide_ref, out_ref, flat_ref, sums_ref = refs[-4:]
-    spread(subs, beams, packed, refs[:-4], wide_ref, flat_ref)
+def first_kernel(subs, beams, packed, bands, step, count, place_any, *refs):
+    wide_ref, out_ref, flat_ref, sums_ref, place_ref, sem = refs[-6:]
+    place_copy = pltpu.make_async_copy(place_any, place_ref, sem)
+    place_copy.start()
+    spread(subs, beams, packed, refs[:-6], wide_ref, flat_ref)
+    place_copy.wait()
     band = partner(lax.axis_index("band"), step, bands)
     add_trials(subs, beams, band * count, count, place_ref, wide_ref, sums_ref, out_ref)
 
@@ -244,8 +251,10 @@
         add_trials(subs, beams, band * count, count, place_ref, wide_ref, refs[-1], out_ref)
 
 
-def peak_kernel(beams, scale, width_ref, *refs):
-    x_refs, (series_ref, peak_ref) = refs[:-2], refs[-2:]
+def peak_kernel(beams, scale, width_any, *refs):
+    x_refs, (series_ref, peak_ref, width_ref, sem) = refs[:-4], refs[-4:]
+    width_copy = pltpu.make_async_copy(width_any, width_ref, sem)
+    width_copy.start()
     blocks, rows, _ = x_refs[0].shape
     per_beam = rows // beams
     series = []
@@ -263,6 +272,7 @@
     left = jnp.concatenate(
         [jnp.concatenate([here, after], axis=1) for here, after in zip(series, following)], axis=0
     )
+    width_copy.wait()
     source = lax.broadcasted_iota(jnp.int32, (2 * LANES, LANES), 0)
     place = lax.broadcasted_iota(jnp.int32, (2 * LANES, LANES), 1)
     for slot in range(peak_ref.shape[1]):
@@ -296,7 +306,7 @@
     chips = sources // 2
     keep, swap = pl.pallas_call(
         functools.partial(fine_kernel, sources),
-        in_specs=[in_smem] + [pl.BlockSpec(memory_space=pl.ANY)] * 2,
+        in_specs=[pl.BlockSpec(memory_space=pl.ANY)] * 3,
         out_specs=[in_vmem] * 2,
         scratch_shapes=[
             pltpu.VMEM((subs, beams, width, block_len), jnp.bfloat16),
@@ -305,7 +315,8 @@
             pltpu.VMEM((1, beams, block_len + MAXD1 + MAXD1 // 2, MAXD1 // 2 * q_count), jnp.float32),
             pltpu.VMEM((subs, beams, block_len + MAXD1 + 8, LANES), jnp.float32),
             pltpu.VMEM((sources, rows - main, LANES), jnp.float32),
-            pltpu.SemaphoreType.DMA((subs + 2,)),
+            pltpu.SMEM(span_start.shape, jnp.int32),
+            pltpu.SemaphoreType.DMA((subs + 3,)),
         ],
         out_shape=[pltpu.VMEM((chips, rows, LANES), jnp.bfloat16)] * 2,
         compiler_params=pltpu.CompilerParams(vmem_limit_bytes=61 << 20),
@@ -328,7 +339,7 @@
         compiler_params=small,
         name="pair_rows",
     )(keep, crossed(swap, 1))
-    received = [pairs[0]] + [crossed(pairs[step], 2 * step) for step in range(1, chips)]
+    received = [crossed(pairs[step], 2 * step) for step in range(chips - 1, 0, -1)] + [pairs[0]]
     stride = round_up(blocks + length // 2 // LANES + 1, 8)
     count = trials // bands
     chunk_shape = (blocks, beams * count, LANES)
@@ -337,9 +348,14 @@
     chunks = [jax.ShapeDtypeStruct(chunk_shape, jnp.bfloat16 if step else jnp.float32) for step in steps]
     wide, first = pl.pallas_call(
         functools.partial(first_kernel, subs, beams, packed, bands, steps[0], count),
-        in_specs=[in_smem] + [in_vmem] * chips,
+        in_specs=[pl.BlockSpec(memory_space=pl.ANY)] + [in_vmem] * chips,
         out_specs=[in_vmem, in_vmem],
-        scratch_shapes=[pltpu.VMEM(((sources + 1) * rows, LANES), jnp.float32), sums_scratch],
+        scratch_shapes=[
+            pltpu.VMEM(((sources + 1) * rows, LANES), jnp.float32),
+            sums_scratch,
+            pltpu.SMEM(places.shape, jnp.int32),
+            pltpu.SemaphoreType.DMA,
+        ],
         out_shape=[jax.ShapeDtypeStruct((subs * beams * QSPAN, stride, LANES), jnp.float32), chunks[0]],
         compiler_params=small,
         name="spread_and_add",
@@ -361,8 +377,9 @@
     arrived = [rest[-1] + arrived[0].astype(jnp.float32)] + arrived[1:]
     series, peaks = pl.pallas_call(
         functools.partial(peak_kernel, beams, math.sqrt(channels * bands)),
-        in_specs=[in_smem] + [in_vmem] * len(arrived),
+        in_specs=[pl.BlockSpec(memory_space=pl.ANY)] + [in_vmem] * len(arrived),
         out_specs=[in_vmem] * 2,
+        scratch_shapes=[pltpu.SMEM(widths.shape, jnp.int32), pltpu.SemaphoreType.DMA],
         out_shape=[
             jax.ShapeDtypeStruct((beams, count, length), jnp.bfloat16),
             jax.ShapeDtypeStruct((beams, widths.shape[0], count), jnp.float32),

time: 38.3 us -> 37.2 us (0.971)
  Pallas kernels: 15.8 us -> 15.2 us
  waiting for transfers between devices: 11.4 us -> 10.8 us
    ppermute x4, waiting for transfers between devices: 5.46 us -> 4.45 us  [crossed(): lax.ppermute(array, 'trial', [(place, place ^ step) for place in range(so...]
    ppermute x3, waiting for transfers between devices: 5.92 us -> 6.34 us  [local(): arrived.append(lax.ppermute(sums, 'band', pairs))]
where the time goes in v4:
time: 37.2 us; the launch traced here: 37 us
  Pallas kernels  15.2 us (41%)
  waiting for transfers between devices  10.8 us (29%)
  starting transfers between devices  9.53 us (26%)
  other arithmetic  0.81 us (2%)
  between operations  0.68 us (2%)
    pallas_call x1, Pallas kernels, local(): pl.pallas_call(functools.partial(fine_kernel, sources), in_specs=[pl.Bloc...  8.99 us
    ppermute x3, waiting for transfers between devices, local(): arrived.append(lax.ppermute(sums, 'band', pairs))  6.34 us
    ppermute x4, starting transfers between devices, crossed(): lax.ppermute(array, 'trial', [(place, place ^ step) for place in range(so...  5.02 us
    ppermute x3, starting transfers between devices, local(): arrived.append(lax.ppermute(sums, 'band', pairs))  4.51 us
    ppermute x4, waiting for transfers between devices, crossed(): lax.ppermute(array, 'trial', [(place, place ^ step) for place in range(so...  4.45 us
    pallas_call x1, Pallas kernels, local(): pl.pallas_call(functools.partial(next_kernel, subs, beams, bands, steps[1...  3.01 us
    pallas_call x1, Pallas kernels, local(): pl.pallas_call(functools.partial(peak_kernel, beams, math.sqrt(channels *...  1.77 us
    pallas_call x1, Pallas kernels, local(): pl.pallas_call(functools.partial(first_kernel, subs, beams, packed, bands...  1.43 us
  transfers between devices with their start and end apart: 7, of which 5 were waited for; matrix products, arithmetic and copies ran while one was open for 2% of the time, Pallas kernels for 8%

profile of v4, /device:TPU:0, one launch (start us, length us, event | category | flops | bytes accessed | tf_op | source)
XLA Modules:
  0.0 37.0 jit_solution(12402967295957694988)
XLA Ops:
  0.6 9.0 %fine_delays.1 = (bf16[4,144,128]{2,1,0:T(8,128)(2,1)S(1)}, bf16[4,144,128]{2,1,0:T(8,128)(2,1)S(1)}) custom-call(s32[8,32]{1,0:T(8,128)} %span_any.1, bf16[2,4096,256]{2,1,0:T(8,128)(2,1)} %x_hbm.1, s32[8,32,512]{2,1,0:T(8,128)} %delay_hbm.1), custom_call_target="tpu_custom_call" | custom-call | tf_op jit(solution)/shard_map/fine_delays/pallas_call | solution.py:307
  9.6 0.5 %collective-permute-start = (bf16[4,144,128]{2,1,0:T(8,128)(2,1)S(1)}, bf16[4,144,128]{2,1,0:T(8,128)(2,1)S(1)}, u32[]{:S(2)}, u32[]{:S(2)}) collective-permute-start(bf16[4,144,128]{2,1,0:T(8,128)(2,1)S(1)} %get-tuple-element.16), channel_id=1, source_target_pairs={{0,1},{1,0},{2,3},{3,2},{4,5},{5,4},{6,7},{7,6},{8,9},{9,8},{10,11... | collective-permute-start | bytes 442376 | tf_op jit(solution)/shard_map/ppermute | solution.py:332
  10.1 1.0 %collective-permute-done.swap_ref = bf16[4,144,128]{2,1,0:T(8,128)(2,1)S(1)} collective-permute-done((bf16[4,144,128]{2,1,0:T(8,128)(2,1)S(1)}, bf16[4,144,128]{2,1,0:T(8,128)(2,1)S(1)}, u32[]{:S(2)}, u32[]{:S(2)}) %collective-permute-start) | collective-permute-done | bytes 147488 | tf_op jit(solution)/shard_map/ppermute | solution.py:332
  11.2 3.9 %collective-permute-start.1 = (bf16[2,144,128]{2,1,0:T(8,128)(2,1)S(1)}, bf16[2,144,128]{2,1,0:T(8,128)(2,1)S(1)}, u32[]{:S(2)}, u32[]{:S(2)}) collective-permute-start(bf16[2,144,128]{2,1,0:T(8,128)(2,1)S(1)} %get-tuple-element.17), channel_id=1, source_target_pairs={{0,6},{1,7},{2,4},{3,5},{4,2},{5,3},{6,0},{7,1},{8,14},{9,15},{10,... | collective-permute-start | bytes 221192 | tf_op jit(solution)/shard_map/ppermute | solution.py:332
  15.0 0.5 %collective-permute-start.2 = (bf16[2,144,128]{2,1,0:T(8,128)(2,1)S(1)}, bf16[2,144,128]{2,1,0:T(8,128)(2,1)S(1)}, u32[]{:S(2)}, u32[]{:S(2)}) collective-permute-start(bf16[2,144,128]{2,1,0:T(8,128)(2,1)S(1)} %get-tuple-element.18), channel_id=1, source_target_pairs={{0,4},{1,5},{2,6},{3,7},{4,0},{5,1},{6,2},{7,3},{8,12},{9,13},{10,... | collective-permute-start | bytes 221192 | tf_op jit(solution)/shard_map/ppermute | solution.py:332
  15.5 0.1 collective-permute-start.3
  15.7 0.8 %add_bitcast_fusion.place_any.place_ref = s32[8,64]{1,0:T(8,128)S(1)} fusion(s32[64,32]{0,1:T(8,128)} %param.10, s32[]{:T(128)S(6)} %select_n.4, s32[64,32]{0,1:T(8,128)} %param.9, s32[8]{0:T(128)S(1)} %iota_multiply_fusion), kind=kLoop, calls=%fused_computation.1 | loop fusion | flops 1536 | bytes 6180 | tf_op jit(solution)/shard_map/add | solution.py:329
  16.5 1.2 %collective-permute-done.1.refs_0_ = bf16[2,144,128]{2,1,0:T(8,128)(2,1)S(1)} collective-permute-done((bf16[2,144,128]{2,1,0:T(8,128)(2,1)S(1)}, bf16[2,144,128]{2,1,0:T(8,128)(2,1)S(1)}, u32[]{:S(2)}, u32[]{:S(2)}) %collective-permute-start.1) | collective-permute-done | bytes 73760 | tf_op jit(solution)/shard_map/ppermute | solution.py:332
  17.7 1.7 %collective-permute-done.2.refs_1_ = bf16[2,144,128]{2,1,0:T(8,128)(2,1)S(1)} collective-permute-done((bf16[2,144,128]{2,1,0:T(8,128)(2,1)S(1)}, bf16[2,144,128]{2,1,0:T(8,128)(2,1)S(1)}, u32[]{:S(2)}, u32[]{:S(2)}) %collective-permute-start.2) | collective-permute-done | bytes 73760 | tf_op jit(solution)/shard_map/ppermute | solution.py:332
  19.4 0.5 %collective-permute-done.3.refs_2_ = bf16[2,144,128]{2,1,0:T(8,128)(2,1)S(1)} collective-permute-done((bf16[2,144,128]{2,1,0:T(8,128)(2,1)S(1)}, bf16[2,144,128]{2,1,0:T(8,128)(2,1)S(1)}, u32[]{:S(2)}, u32[]{:S(2)}) %collective-permute-start.3) | collective-permute-done | bytes 73760 | tf_op jit(solution)/shard_map/ppermute | solution.py:332
  19.9 1.4 %spread_and_add.1 = (f32[64,32,128]{2,1,0:T(8,128)S(1)}, bf16[16,32,128]{2,1,0:T(8,128)(2,1)S(1)}) custom-call(s32[8,64]{1,0:T(8,128)S(1)} %add_bitcast_fusion.place_any.place_ref, bf16[2,144,128]{2,1,0:T(8,128)(2,1)S(1)} %collective-permute-done.1.refs_0_, bf16[2,144,128]{2,1,0:T(8,128)(2,1)S(1)} %collective-permute-done.2.refs_1_, ...), custom_call_target="tpu_custom_call" | custom-call | tf_op jit(solution)/shard_map/spread_and_add/pallas_call | solution.py:349
  21.3 3.7 %collective-permute-start.4 = (bf16[16,32,128]{2,1,0:T(8,128)(2,1)S(1)}, bf16[16,32,128]{2,1,0:T(8,128)(2,1)S(1)}, u32[]{:S(2)}, u32[]{:S(2)}) collective-permute-start(bf16[16,32,128]{2,1,0:T(8,128)(2,1)S(1)} %get-tuple-element.23), channel_id=1, source_target_pairs={{0,24},{8,16},{16,8},{24,0},{1,25},{9,17},{17,9},{25,1},{2,26},{10... | collective-permute-start | bytes 393224 | tf_op jit(solution)/shard_map/ppermute | solution.py:376
  25.0 0.0 copy-start
  25.0 3.0 %add_trials.1 = (bf16[16,32,128]{2,1,0:T(8,128)(2,1)S(1)}, bf16[16,32,128]{2,1,0:T(8,128)(2,1)S(1)}, f32[16,32,128]{2,1,0:T(8,128)S(1)}) custom-call(s32[8,64]{1,0:T(8,128)S(1)} %add_bitcast_fusion.place_any.place_ref, f32[64,32,128]{2,1,0:T(8,128)S(1)} %get-tuple-element.21.wide_ref), custom_call_target="tpu_custom_call" | custom-call | flops 4294967296 | bytes 12582912 | tf_op jit(solution)/shard_map/add_trials/pallas_call | solution.py:363
  28.0 0.1 collective-permute-start.5
  28.1 0.8 %collective-permute-start.6 = (bf16[16,32,128]{2,1,0:T(8,128)(2,1)S(1)}, bf16[16,32,128]{2,1,0:T(8,128)(2,1)S(1)}, u32[]{:S(2)}, u32[]{:S(2)}) collective-permute-start(bf16[16,32,128]{2,1,0:T(8,128)(2,1)S(1)} %get-tuple-element.25), channel_id=1, source_target_pairs={{0,8},{8,0},{16,24},{24,16},{1,9},{9,1},{17,25},{25,17},{2,10},{10... | collective-permute-start | bytes 393224 | tf_op jit(solution)/shard_map/ppermute | solution.py:376
  28.9 0.0 collective-permute-done.4
  28.9 6.3 %collective-permute-done.5.refs_1_ = bf16[16,32,128]{2,1,0:T(8,128)(2,1)S(1)} collective-permute-done((bf16[16,32,128]{2,1,0:T(8,128)(2,1)S(1)}, bf16[16,32,128]{2,1,0:T(8,128)(2,1)S(1)}, u32[]{:S(2)}, u32[]{:S(2)}) %collective-permute-start.5) | collective-permute-done | bytes 131104 | tf_op jit(solution)/shard_map/ppermute | solution.py:376
  35.2 0.0 collective-permute-done.6.refs_2_
  35.3 0.0 copy-done
  35.3 1.8 %boxcar_peaks.1 = (bf16[2,16,2048]{2,1,0:T(8,128)(2,1)}, f32[2,4,16]{2,1,0:T(4,128)}) custom-call(s32[4]{0:T(128)S(1)} %copy-done, f32[16,32,128]{2,1,0:T(8,128)S(1)} %convert_add_fusion.refs_0_, bf16[16,32,128]{2,1,0:T(8,128)(2,1)S(1)} %collective-permute-done.5.refs_1_, bf16[16,32,128]{2,1,0:T(8,128)(2,1)S(1)} %collective-permute-done.6.refs_2_), custom_call_target="tpu_custom_call" | custom-call | tf_op jit(solution)/shard_map/boxcar_peaks/pallas_call | solution.py:378
  (3 shorter events, 0.1 us)
Async XLA Ops:
  9.6 1.5 %collective-permute-start = (bf16[4,144,128]{2,1,0:T(8,128)(2,1)S(1)}, bf16[4,144,128]{2,1,0:T(8,128)(2,1)S(1)}, u32[]{:S(2)}, u32[]{:S(2)}) collective-permute-start(bf16[4,144,128]{2,1,0:T(8,128)(2,1)S(1)} %get-tuple-element.16), channel_id=1, source_target_pairs={{0,1},{1,0},{2,3},{3,2},{4,5},{5,4},{6,7},{7,6},{8,9},{9,8},{10,11... | collective-permute-start | bytes 442376 | tf_op jit(solution)/shard_map/ppermute | solution.py:332
  11.2 6.5 %collective-permute-start.1 = (bf16[2,144,128]{2,1,0:T(8,128)(2,1)S(1)}, bf16[2,144,128]{2,1,0:T(8,128)(2,1)S(1)}, u32[]{:S(2)}, u32[]{:S(2)}) collective-permute-start(bf16[2,144,128]{2,1,0:T(8,128)(2,1)S(1)} %get-tuple-element.17), channel_id=1, source_target_pairs={{0,6},{1,7},{2,4},{3,5},{4,2},{5,3},{6,0},{7,1},{8,14},{9,15},{10,... | collective-permute-start | bytes 221192 | tf_op jit(solution)/shard_map/ppermute | solution.py:332
  15.0 4.4 %collective-permute-start.2 = (bf16[2,144,128]{2,1,0:T(8,128)(2,1)S(1)}, bf16[2,144,128]{2,1,0:T(8,128)(2,1)S(1)}, u32[]{:S(2)}, u32[]{:S(2)}) collective-permute-start(bf16[2,144,128]{2,1,0:T(8,128)(2,1)S(1)} %get-tuple-element.18), channel_id=1, source_target_pairs={{0,4},{1,5},{2,6},{3,7},{4,0},{5,1},{6,2},{7,3},{8,12},{9,13},{10,... | collective-permute-start | bytes 221192 | tf_op jit(solution)/shard_map/ppermute | solution.py:332
  15.5 4.4 %collective-permute-start.3 = (bf16[2,144,128]{2,1,0:T(8,128)(2,1)S(1)}, bf16[2,144,128]{2,1,0:T(8,128)(2,1)S(1)}, u32[]{:S(2)}, u32[]{:S(2)}) collective-permute-start(bf16[2,144,128]{2,1,0:T(8,128)(2,1)S(1)} %get-tuple-element.19), channel_id=1, source_target_pairs={{0,2},{1,3},{2,0},{3,1},{4,6},{5,7},{6,4},{7,5},{8,10},{9,11},{10,... | collective-permute-start | bytes 221192 | tf_op jit(solution)/shard_map/ppermute | solution.py:332
  21.3 7.5 %collective-permute-start.4 = (bf16[16,32,128]{2,1,0:T(8,128)(2,1)S(1)}, bf16[16,32,128]{2,1,0:T(8,128)(2,1)S(1)}, u32[]{:S(2)}, u32[]{:S(2)}) collective-permute-start(bf16[16,32,128]{2,1,0:T(8,128)(2,1)S(1)} %get-tuple-element.23), channel_id=1, source_target_pairs={{0,24},{8,16},{16,8},{24,0},{1,25},{9,17},{17,9},{25,1},{2,26},{10... | collective-permute-start | bytes 393224 | tf_op jit(solution)/shard_map/ppermute | solution.py:376
  25.0 10.2 %copy-start = (s32[4]{0:T(128)S(1)}, s32[4]{0:T(128)}, u32[]{:S(2)}) copy-start(s32[4]{0:T(128)} %width_any.1) | copy-start | bytes 52
  28.0 7.2 %collective-permute-start.5 = (bf16[16,32,128]{2,1,0:T(8,128)(2,1)S(1)}, bf16[16,32,128]{2,1,0:T(8,128)(2,1)S(1)}, u32[]{:S(2)}, u32[]{:S(2)}) collective-permute-start(bf16[16,32,128]{2,1,0:T(8,128)(2,1)S(1)} %get-tuple-element.24), channel_id=1, source_target_pairs={{0,16},{8,24},{16,0},{24,8},{1,17},{9,25},{17,1},{25,9},{2,18},{10... | collective-permute-start | bytes 393224 | tf_op jit(solution)/shard_map/ppermute | solution.py:376
  28.1 7.1 %collective-permute-start.6 = (bf16[16,32,128]{2,1,0:T(8,128)(2,1)S(1)}, bf16[16,32,128]{2,1,0:T(8,128)(2,1)S(1)}, u32[]{:S(2)}, u32[]{:S(2)}) collective-permute-start(bf16[16,32,128]{2,1,0:T(8,128)(2,1)S(1)} %get-tuple-element.25), channel_id=1, source_target_pairs={{0,8},{8,0},{16,24},{24,16},{1,9},{9,1},{17,25},{25,17},{2,10},{10... | collective-permute-start | bytes 393224 | tf_op jit(solution)/shard_map/ppermute | solution.py:376

commit v5 on v4

--- a/solution.py
+++ b/solution.py
@@ -345,7 +345,6 @@
     chunk_shape = (blocks, beams * count, LANES)
     sums_scratch = pltpu.VMEM((blocks * beams * count, LANES), jnp.float32)
     steps = list(range(bands - 1, -1, -1))
-    chunks = [jax.ShapeDtypeStruct(chunk_shape, jnp.bfloat16 if step else jnp.float32) for step in steps]
     wide, first = pl.pallas_call(
         functools.partial(first_kernel, subs, beams, packed, bands, steps[0], count),
         in_specs=[pl.BlockSpec(memory_space=pl.ANY)] + [in_vmem] * chips,
@@ -356,25 +355,32 @@
             pltpu.SMEM(places.shape, jnp.int32),
             pltpu.SemaphoreType.DMA,
         ],
-        out_shape=[jax.ShapeDtypeStruct((subs * beams * QSPAN, stride, LANES), jnp.float32), chunks[0]],
+        out_shape=[jax.ShapeDtypeStruct((subs * beams * QSPAN, stride, LANES), jnp.float32), jax.ShapeDtypeStruct(chunk_shape, jnp.bfloat16)],
         compiler_params=small,
         name="spread_and_add",
     )(places, *received)
+    later = steps[1:]
+    kinds = [jnp.bfloat16 if step % 2 else jnp.float32 for step in later]
     rest = pl.pallas_call(
-        functools.partial(next_kernel, subs, beams, bands, steps[1:], count),
+        functools.partial(next_kernel, subs, beams, bands, later, count),
         in_specs=[in_smem, in_vmem],
-        out_specs=[in_vmem] * (bands - 1),
+        out_specs=[in_vmem] * len(later),
         scratch_shapes=[sums_scratch],
-        out_shape=chunks[1:],
+        out_shape=[jax.ShapeDtypeStruct(chunk_shape, kind) for kind in kinds],
         compiler_params=small,
         cost_estimate=pl.CostEstimate(flops=4 << 30, bytes_accessed=12 << 20, transcendentals=0),
         name="add_trials",
     )(places, wide)
-    arrived = []
-    for step, sums in zip(steps[:-1], [first] + list(rest[:-1])):
-        pairs = [(place, partner(place, step, bands)) for place in range(bands)]
-        arrived.append(lax.ppermute(sums, "band", pairs))
-    arrived = [rest[-1] + arrived[0].astype(jnp.float32)] + arrived[1:]
+
+    def sent(sums, step):
+        return lax.ppermute(sums, "band", [(place, partner(place, step, bands)) for place in range(bands)])
+
+    chunks = dict(zip(steps, [first] + list(rest)))
+    arrived = [chunks[0]]
+    for step in range(2, bands, 2):
+        from_pair = sent(chunks[step + 1], 1).astype(jnp.float32)
+        arrived.append(sent((chunks[step] + from_pair).astype(jnp.bfloat16), step))
+    arrived.append(sent(chunks[1], 1))
     series, peaks = pl.pallas_call(
         functools.partial(peak_kernel, beams, math.sqrt(channels * bands)),
         in_specs=[pl.BlockSpec(memory_space=pl.ANY)] + [in_vmem] * len(arrived),

time: 37.2 us -> 35.5 us (0.954)
  waiting for transfers between devices: 10.8 us -> 8.76 us
    ppermute x3, waiting for transfers between devices: 6.34 us -> 4.32 us  [sent(): lax.ppermute(sums, 'band', [(place, partner(place, step, bands)) for plac...]
  transfers between devices with their start and end apart: 7 -> 7, of which waited for: 5 -> 6; matrix products, arithmetic and copies ran while one was open for 2% -> 2% of each run, Pallas kernels for 8% -> 9%
where the time goes in v5:
time: 35.5 us; the launch traced here: 35.3 us
  Pallas kernels  15.2 us (43%)
  starting transfers between devices  9.83 us (28%)
  waiting for transfers between devices  8.76 us (25%)
  other arithmetic  0.81 us (2%)
  between operations  0.67 us (2%)
    pallas_call x1, Pallas kernels, local(): pl.pallas_call(functools.partial(fine_kernel, sources), in_specs=[pl.Bloc...  8.99 us
    ppermute x4, starting transfers between devices, crossed(): lax.ppermute(array, 'trial', [(place, place ^ step) for place in range(so...  5.02 us
    ppermute x3, starting transfers between devices, sent(): lax.ppermute(sums, 'band', [(place, partner(place, step, bands)) for plac...  4.81 us
    ppermute x4, waiting for transfers between devices, crossed(): lax.ppermute(array, 'trial', [(place, place ^ step) for place in range(so...  4.45 us
    ppermute x3, waiting for transfers between devices, sent(): lax.ppermute(sums, 'band', [(place, partner(place, step, bands)) for plac...  4.32 us
    pallas_call x1, Pallas kernels, local(): pl.pallas_call(functools.partial(next_kernel, subs, beams, bands, later,...  3.01 us
    pallas_call x1, Pallas kernels, local(): pl.pallas_call(functools.partial(peak_kernel, beams, math.sqrt(channels *...  1.77 us
    pallas_call x1, Pallas kernels, local(): pl.pallas_call(functools.partial(first_kernel, subs, beams, packed, bands...  1.43 us
  transfers between devices with their start and end apart: 7, of which 6 were waited for; matrix products, arithmetic and copies ran while one was open for 2% of the time, Pallas kernels for 9%

profile of v5, /device:TPU:0, one launch (start us, length us, event | category | flops | bytes accessed | tf_op | source)
XLA Modules:
  0.0 35.3 jit_solution(11523303346307661732)
XLA Ops:
  0.6 9.0 %fine_delays.1 = (bf16[4,144,128]{2,1,0:T(8,128)(2,1)S(1)}, bf16[4,144,128]{2,1,0:T(8,128)(2,1)S(1)}) custom-call(s32[8,32]{1,0:T(8,128)} %span_any.1, bf16[2,4096,256]{2,1,0:T(8,128)(2,1)} %x_hbm.1, s32[8,32,512]{2,1,0:T(8,128)} %delay_hbm.1), custom_call_target="tpu_custom_call" | custom-call | tf_op jit(solution)/shard_map/fine_delays/pallas_call | solution.py:307
  9.6 0.5 %collective-permute-start = (bf16[4,144,128]{2,1,0:T(8,128)(2,1)S(1)}, bf16[4,144,128]{2,1,0:T(8,128)(2,1)S(1)}, u32[]{:S(2)}, u32[]{:S(2)}) collective-permute-start(bf16[4,144,128]{2,1,0:T(8,128)(2,1)S(1)} %get-tuple-element.16), channel_id=1, source_target_pairs={{0,1},{1,0},{2,3},{3,2},{4,5},{5,4},{6,7},{7,6},{8,9},{9,8},{10,11... | collective-permute-start | bytes 442376 | tf_op jit(solution)/shard_map/ppermute | solution.py:332
  10.1 1.0 %collective-permute-done.swap_ref = bf16[4,144,128]{2,1,0:T(8,128)(2,1)S(1)} collective-permute-done((bf16[4,144,128]{2,1,0:T(8,128)(2,1)S(1)}, bf16[4,144,128]{2,1,0:T(8,128)(2,1)S(1)}, u32[]{:S(2)}, u32[]{:S(2)}) %collective-permute-start) | collective-permute-done | bytes 147488 | tf_op jit(solution)/shard_map/ppermute | solution.py:332
  11.2 3.9 %collective-permute-start.1 = (bf16[2,144,128]{2,1,0:T(8,128)(2,1)S(1)}, bf16[2,144,128]{2,1,0:T(8,128)(2,1)S(1)}, u32[]{:S(2)}, u32[]{:S(2)}) collective-permute-start(bf16[2,144,128]{2,1,0:T(8,128)(2,1)S(1)} %get-tuple-element.17), channel_id=1, source_target_pairs={{0,6},{1,7},{2,4},{3,5},{4,2},{5,3},{6,0},{7,1},{8,14},{9,15},{10,... | collective-permute-start | bytes 221192 | tf_op jit(solution)/shard_map/ppermute | solution.py:332
  15.0 0.5 %collective-permute-start.2 = (bf16[2,144,128]{2,1,0:T(8,128)(2,1)S(1)}, bf16[2,144,128]{2,1,0:T(8,128)(2,1)S(1)}, u32[]{:S(2)}, u32[]{:S(2)}) collective-permute-start(bf16[2,144,128]{2,1,0:T(8,128)(2,1)S(1)} %get-tuple-element.18), channel_id=1, source_target_pairs={{0,4},{1,5},{2,6},{3,7},{4,0},{5,1},{6,2},{7,3},{8,12},{9,13},{10,... | collective-permute-start | bytes 221192 | tf_op jit(solution)/shard_map/ppermute | solution.py:332
  15.5 0.1 collective-permute-start.3
  15.7 0.8 %add_bitcast_fusion.place_any.place_ref = s32[8,64]{1,0:T(8,128)S(1)} fusion(s32[64,32]{0,1:T(8,128)} %param.10, s32[]{:T(128)S(6)} %select_n.4, s32[64,32]{0,1:T(8,128)} %param.9, s32[8]{0:T(128)S(1)} %iota_multiply_fusion), kind=kLoop, calls=%fused_computation.1 | loop fusion | flops 1536 | bytes 6180 | tf_op jit(solution)/shard_map/add | solution.py:329
  16.5 1.2 %collective-permute-done.1.refs_0_ = bf16[2,144,128]{2,1,0:T(8,128)(2,1)S(1)} collective-permute-done((bf16[2,144,128]{2,1,0:T(8,128)(2,1)S(1)}, bf16[2,144,128]{2,1,0:T(8,128)(2,1)S(1)}, u32[]{:S(2)}, u32[]{:S(2)}) %collective-permute-start.1) | collective-permute-done | bytes 73760 | tf_op jit(solution)/shard_map/ppermute | solution.py:332
  17.7 1.7 %collective-permute-done.2.refs_1_ = bf16[2,144,128]{2,1,0:T(8,128)(2,1)S(1)} collective-permute-done((bf16[2,144,128]{2,1,0:T(8,128)(2,1)S(1)}, bf16[2,144,128]{2,1,0:T(8,128)(2,1)S(1)}, u32[]{:S(2)}, u32[]{:S(2)}) %collective-permute-start.2) | collective-permute-done | bytes 73760 | tf_op jit(solution)/shard_map/ppermute | solution.py:332
  19.4 0.5 %collective-permute-done.3.refs_2_ = bf16[2,144,128]{2,1,0:T(8,128)(2,1)S(1)} collective-permute-done((bf16[2,144,128]{2,1,0:T(8,128)(2,1)S(1)}, bf16[2,144,128]{2,1,0:T(8,128)(2,1)S(1)}, u32[]{:S(2)}, u32[]{:S(2)}) %collective-permute-start.3) | collective-permute-done | bytes 73760 | tf_op jit(solution)/shard_map/ppermute | solution.py:332
  19.9 1.4 %spread_and_add.1 = (f32[64,32,128]{2,1,0:T(8,128)S(1)}, bf16[16,32,128]{2,1,0:T(8,128)(2,1)S(1)}) custom-call(s32[8,64]{1,0:T(8,128)S(1)} %add_bitcast_fusion.place_any.place_ref, bf16[2,144,128]{2,1,0:T(8,128)(2,1)S(1)} %collective-permute-done.1.refs_0_, bf16[2,144,128]{2,1,0:T(8,128)(2,1)S(1)} %collective-permute-done.2.refs_1_, ...), custom_call_target="tpu_custom_call" | custom-call | tf_op jit(solution)/shard_map/spread_and_add/pallas_call | solution.py:348
  21.3 1.7 %collective-permute-start.4 = (bf16[16,32,128]{2,1,0:T(8,128)(2,1)S(1)}, bf16[16,32,128]{2,1,0:T(8,128)(2,1)S(1)}, u32[]{:S(2)}, u32[]{:S(2)}) collective-permute-start(bf16[16,32,128]{2,1,0:T(8,128)(2,1)S(1)} %get-tuple-element.24), channel_id=1, source_target_pairs={{0,8},{8,0},{16,24},{24,16},{1,9},{9,1},{17,25},{25,17},{2,10},{10... | collective-permute-start | bytes 393224 | tf_op jit(solution)/shard_map/ppermute | solution.py:376
  23.0 0.0 copy-start
  23.0 3.0 %add_trials.1 = (f32[16,32,128]{2,1,0:T(8,128)S(1)}, bf16[16,32,128]{2,1,0:T(8,128)(2,1)S(1)}, f32[16,32,128]{2,1,0:T(8,128)S(1)}) custom-call(s32[8,64]{1,0:T(8,128)S(1)} %add_bitcast_fusion.place_any.place_ref, f32[64,32,128]{2,1,0:T(8,128)S(1)} %get-tuple-element.21.wide_ref), custom_call_target="tpu_custom_call" | custom-call | flops 4294967296 | bytes 12582912 | tf_op jit(solution)/shard_map/add_trials/pallas_call | solution.py:364
  26.0 0.5 %collective-permute-start.6 = (bf16[16,32,128]{2,1,0:T(8,128)(2,1)S(1)}, bf16[16,32,128]{2,1,0:T(8,128)(2,1)S(1)}, u32[]{:S(2)}, u32[]{:S(2)}) collective-permute-start(bf16[16,32,128]{2,1,0:T(8,128)(2,1)S(1)} %get-tuple-element.25), channel_id=1, source_target_pairs={{0,8},{8,0},{16,24},{24,16},{1,9},{9,1},{17,25},{25,17},{2,10},{10... | collective-permute-start | bytes 393224 | tf_op jit(solution)/shard_map/ppermute | solution.py:376
  26.5 0.0 collective-permute-done.4
  26.6 2.7 %collective-permute-start.5 = (bf16[16,32,128]{2,1,0:T(8,128)(2,1)S(1)}, bf16[16,32,128]{2,1,0:T(8,128)(2,1)S(1)}, u32[]{:S(2)}, u32[]{:S(2)}) collective-permute-start(bf16[16,32,128]{2,1,0:T(8,128)(2,1)S(1)} %add_convert_fusion), channel_id=1, source_target_pairs={{0,16},{8,24},{16,0},{24,8},{1,17},{9,25},{17,1},{25,9},{2,18},{10... | collective-permute-start | bytes 393224 | tf_op jit(solution)/shard_map/ppermute | solution.py:376
  29.2 2.3 %collective-permute-done.6.refs_2_ = bf16[16,32,128]{2,1,0:T(8,128)(2,1)S(1)} collective-permute-done((bf16[16,32,128]{2,1,0:T(8,128)(2,1)S(1)}, bf16[16,32,128]{2,1,0:T(8,128)(2,1)S(1)}, u32[]{:S(2)}, u32[]{:S(2)}) %collective-permute-start.6) | collective-permute-done | bytes 131104 | tf_op jit(solution)/shard_map/ppermute | solution.py:376
  31.5 2.0 %collective-permute-done.5.refs_1_ = bf16[16,32,128]{2,1,0:T(8,128)(2,1)S(1)} collective-permute-done((bf16[16,32,128]{2,1,0:T(8,128)(2,1)S(1)}, bf16[16,32,128]{2,1,0:T(8,128)(2,1)S(1)}, u32[]{:S(2)}, u32[]{:S(2)}) %collective-permute-start.5) | collective-permute-done | bytes 131104 | tf_op jit(solution)/shard_map/ppermute | solution.py:376
  33.5 0.0 copy-done
  33.5 1.8 %boxcar_peaks.1 = (bf16[2,16,2048]{2,1,0:T(8,128)(2,1)}, f32[2,4,16]{2,1,0:T(4,128)}) custom-call(s32[4]{0:T(128)S(1)} %copy-done, f32[16,32,128]{2,1,0:T(8,128)S(1)} %get-tuple-element.22.refs_0_, bf16[16,32,128]{2,1,0:T(8,128)(2,1)S(1)} %collective-permute-done.5.refs_1_, bf16[16,32,128]{2,1,0:T(8,128)(2,1)S(1)} %collective-permute-done.6.refs_2_), custom_call_target="tpu_custom_call" | custom-call | tf_op jit(solution)/shard_map/boxcar_peaks/pallas_call | solution.py:384
  (3 shorter events, 0.1 us)
Async XLA Ops:
  9.6 1.5 %collective-permute-start = (bf16[4,144,128]{2,1,0:T(8,128)(2,1)S(1)}, bf16[4,144,128]{2,1,0:T(8,128)(2,1)S(1)}, u32[]{:S(2)}, u32[]{:S(2)}) collective-permute-start(bf16[4,144,128]{2,1,0:T(8,128)(2,1)S(1)} %get-tuple-element.16), channel_id=1, source_target_pairs={{0,1},{1,0},{2,3},{3,2},{4,5},{5,4},{6,7},{7,6},{8,9},{9,8},{10,11... | collective-permute-start | bytes 442376 | tf_op jit(solution)/shard_map/ppermute | solution.py:332
  11.2 6.5 %collective-permute-start.1 = (bf16[2,144,128]{2,1,0:T(8,128)(2,1)S(1)}, bf16[2,144,128]{2,1,0:T(8,128)(2,1)S(1)}, u32[]{:S(2)}, u32[]{:S(2)}) collective-permute-start(bf16[2,144,128]{2,1,0:T(8,128)(2,1)S(1)} %get-tuple-element.17), channel_id=1, source_target_pairs={{0,6},{1,7},{2,4},{3,5},{4,2},{5,3},{6,0},{7,1},{8,14},{9,15},{10,... | collective-permute-start | bytes 221192 | tf_op jit(solution)/shard_map/ppermute | solution.py:332
  15.0 4.4 %collective-permute-start.2 = (bf16[2,144,128]{2,1,0:T(8,128)(2,1)S(1)}, bf16[2,144,128]{2,1,0:T(8,128)(2,1)S(1)}, u32[]{:S(2)}, u32[]{:S(2)}) collective-permute-start(bf16[2,144,128]{2,1,0:T(8,128)(2,1)S(1)} %get-tuple-element.18), channel_id=1, source_target_pairs={{0,4},{1,5},{2,6},{3,7},{4,0},{5,1},{6,2},{7,3},{8,12},{9,13},{10,... | collective-permute-start | bytes 221192 | tf_op jit(solution)/shard_map/ppermute | solution.py:332
  15.5 4.4 %collective-permute-start.3 = (bf16[2,144,128]{2,1,0:T(8,128)(2,1)S(1)}, bf16[2,144,128]{2,1,0:T(8,128)(2,1)S(1)}, u32[]{:S(2)}, u32[]{:S(2)}) collective-permute-start(bf16[2,144,128]{2,1,0:T(8,128)(2,1)S(1)} %get-tuple-element.19), channel_id=1, source_target_pairs={{0,2},{1,3},{2,0},{3,1},{4,6},{5,7},{6,4},{7,5},{8,10},{9,11},{10,... | collective-permute-start | bytes 221192 | tf_op jit(solution)/shard_map/ppermute | solution.py:332
  21.3 5.2 %collective-permute-start.4 = (bf16[16,32,128]{2,1,0:T(8,128)(2,1)S(1)}, bf16[16,32,128]{2,1,0:T(8,128)(2,1)S(1)}, u32[]{:S(2)}, u32[]{:S(2)}) collective-permute-start(bf16[16,32,128]{2,1,0:T(8,128)(2,1)S(1)} %get-tuple-element.24), channel_id=1, source_target_pairs={{0,8},{8,0},{16,24},{24,16},{1,9},{9,1},{17,25},{25,17},{2,10},{10... | collective-permute-start | bytes 393224 | tf_op jit(solution)/shard_map/ppermute | solution.py:376
  23.0 10.5 %copy-start = (s32[4]{0:T(128)S(1)}, s32[4]{0:T(128)}, u32[]{:S(2)}) copy-start(s32[4]{0:T(128)} %width_any.1) | copy-start | bytes 52
  26.0 5.5 %collective-permute-start.6 = (bf16[16,32,128]{2,1,0:T(8,128)(2,1)S(1)}, bf16[16,32,128]{2,1,0:T(8,128)(2,1)S(1)}, u32[]{:S(2)}, u32[]{:S(2)}) collective-permute-start(bf16[16,32,128]{2,1,0:T(8,128)(2,1)S(1)} %get-tuple-element.25), channel_id=1, source_target_pairs={{0,8},{8,0},{16,24},{24,16},{1,9},{9,1},{17,25},{25,17},{2,10},{10... | collective-permute-start | bytes 393224 | tf_op jit(solution)/shard_map/ppermute | solution.py:376
  26.6 7.0 %collective-permute-start.5 = (bf16[16,32,128]{2,1,0:T(8,128)(2,1)S(1)}, bf16[16,32,128]{2,1,0:T(8,128)(2,1)S(1)}, u32[]{:S(2)}, u32[]{:S(2)}) collective-permute-start(bf16[16,32,128]{2,1,0:T(8,128)(2,1)S(1)} %add_convert_fusion), channel_id=1, source_target_pairs={{0,16},{8,24},{16,0},{24,8},{1,17},{9,25},{17,1},{25,9},{2,18},{10... | collective-permute-start | bytes 393224 | tf_op jit(solution)/shard_map/ppermute | solution.py:376

commit v6 on v5

--- a/solution.py
+++ b/solution.py
@@ -227,27 +227,27 @@
                 sums_ref[pl.ds(start, 8, stride=beams * count), :] = sums[beam][part]
         return carry
 
-    lax.fori_loop(0, count, one_trial, 0, unroll=min(count, 8))
+    lax.fori_loop(0, count, one_trial, 0, unroll=min(count, 16))
     out_ref[...] = sums_ref[...].reshape(out_ref.shape).astype(out_ref.dtype)
 
 
-def partner(place, step, peers):
-    return place ^ step if peers & (peers - 1) == 0 else (place + step) % peers
-
-
-def first_kernel(subs, beams, packed, bands, step, count, place_any, *refs):
+def partner(place, step):
+    return place ^ step
+
+
+def first_kernel(subs, beams, packed, step, count, place_any, *refs):
     wide_ref, out_ref, flat_ref, sums_ref, place_ref, sem = refs[-6:]
     place_copy = pltpu.make_async_copy(place_any, place_ref, sem)
     place_copy.start()
     spread(subs, beams, packed, refs[:-6], wide_ref, flat_ref)
     place_copy.wait()
-    band = partner(lax.axis_index("band"), step, bands)
+    band = partner(lax.axis_index("band"), step)
     add_trials(subs, beams, band * count, count, place_ref, wide_ref, sums_ref, out_ref)
 
 
-def next_kernel(subs, beams, bands, steps, count, place_ref, wide_ref, *refs):
+def next_kernel(subs, beams, steps, count, place_ref, wide_ref, *refs):
     for step, out_ref in zip(steps, refs):
-        band = partner(lax.axis_index("band"), step, bands)
+        band = partner(lax.axis_index("band"), step)
         add_trials(subs, beams, band * count, count, place_ref, wide_ref, refs[-1], out_ref)
 
 
@@ -275,15 +275,23 @@
     width_copy.wait()
     source = lax.broadcasted_iota(jnp.int32, (2 * LANES, LANES), 0)
     place = lax.broadcasted_iota(jnp.int32, (2 * LANES, LANES), 1)
-    for slot in range(peak_ref.shape[1]):
-        width = width_ref[slot]
-        window = ((source >= place) & (source < place + width)).astype(jnp.bfloat16)
-        totals = jnp.dot(left, window, preferred_element_type=jnp.float32)
-        best = totals[:rows]
-        for block in range(1, blocks):
-            best = jnp.maximum(best, totals[block * rows : (block + 1) * rows])
-        root = jnp.sqrt(jnp.full((1, rows), width, jnp.int32).astype(jnp.float32))
-        peaks = jnp.max(best.T, axis=0, keepdims=True) / root
+    slots = peak_ref.shape[1]
+    window = jnp.concatenate(
+        [
+            jnp.where((source >= place) & (source < place + width_ref[slot]), 1.0, 0.0).astype(jnp.bfloat16)
+            for slot in range(slots)
+        ],
+        axis=1,
+    )
+    best = None
+    for block in range(0, blocks, 4):
+        totals = jnp.dot(left[block * rows : (block + 4) * rows], window, preferred_element_type=jnp.float32)
+        for inside in range(4):
+            piece = totals[inside * rows : (inside + 1) * rows]
+            best = piece if best is None else jnp.maximum(best, piece)
+    for slot in range(slots):
+        root = jnp.sqrt(jnp.full((1, rows), width_ref[slot], jnp.int32).astype(jnp.float32))
+        peaks = jnp.max(best[:, slot * LANES : (slot + 1) * LANES].T, axis=0, keepdims=True) / root
         for beam in range(beams):
             peak_ref[beam, slot : slot + 1, :] = peaks[:, beam * per_beam : (beam + 1) * per_beam]
 
@@ -346,7 +354,7 @@
     sums_scratch = pltpu.VMEM((blocks * beams * count, LANES), jnp.float32)
     steps = list(range(bands - 1, -1, -1))
     wide, first = pl.pallas_call(
-        functools.partial(first_kernel, subs, beams, packed, bands, steps[0], count),
+        functools.partial(first_kernel, subs, beams, packed, steps[0], count),
         in_specs=[pl.BlockSpec(memory_space=pl.ANY)] + [in_vmem] * chips,
         out_specs=[in_vmem, in_vmem],
         scratch_shapes=[
@@ -359,24 +367,23 @@
         compiler_params=small,
         name="spread_and_add",
     )(places, *received)
-    later = steps[1:]
-    kinds = [jnp.bfloat16 if step % 2 else jnp.float32 for step in later]
-    rest = pl.pallas_call(
-        functools.partial(next_kernel, subs, beams, bands, later, count),
-        in_specs=[in_smem, in_vmem],
-        out_specs=[in_vmem] * len(later),
-        scratch_shapes=[sums_scratch],
-        out_shape=[jax.ShapeDtypeStruct(chunk_shape, kind) for kind in kinds],
-        compiler_params=small,
-        cost_estimate=pl.CostEstimate(flops=4 << 30, bytes_accessed=12 << 20, transcendentals=0),
-        name="add_trials",
-    )(places, wide)
+    def more(some):
+        return pl.pallas_call(
+            functools.partial(next_kernel, subs, beams, some, count),
+            in_specs=[in_smem, in_vmem],
+            out_specs=[in_vmem] * len(some),
+            scratch_shapes=[sums_scratch],
+            out_shape=[jax.ShapeDtypeStruct(chunk_shape, jnp.bfloat16 if step % 2 else jnp.float32) for step in some],
+            compiler_params=small,
+            cost_estimate=pl.CostEstimate(flops=len(some) << 30, bytes_accessed=len(some) << 22, transcendentals=0),
+            name="add_trials",
+        )(places, wide)
 
     def sent(sums, step):
-        return lax.ppermute(sums, "band", [(place, partner(place, step, bands)) for place in range(bands)])
-
-    chunks = dict(zip(steps, [first] + list(rest)))
-    arrived = [chunks[0]]
+        return lax.ppermute(sums, "band", [(place, partner(place, step)) for place in range(bands)])
+
+    chunks = dict(zip(steps, [first] + list(more(steps[1:-1]))))
+    arrived = list(more([0]))
     for step in range(2, bands, 2):
         from_pair = sent(chunks[step + 1], 1).astype(jnp.float32)
         arrived.append(sent((chunks[step] + from_pair).astype(jnp.bfloat16), step))

time: 35.5 us -> 35.2 us (level); the launches traced: 35.3 us -> 34.5 us
  waiting for transfers between devices: 8.76 us -> 7.89 us
    ppermute x3, waiting for transfers between devices: 4.32 us -> 3.45 us  [sent(): lax.ppermute(sums, 'band', [(place, partner(place, step)) for place in ra...]
    pallas_call x2 -> x3, Pallas kernels: 4.44 us -> 4.6 us  [the longest x2 3.27 us: more(): pl.pallas_call(functools.partial(next_kernel, subs, beams, some, count),...]
where the time goes in v6:
time: 35.2 us; the launch traced here: 34.5 us
  Pallas kernels  15.3 us (43%)
  starting transfers between devices  9.82 us (28%)
  waiting for transfers between devices  7.89 us (22%)
  other arithmetic  0.81 us (2%)
  between operations  0.69 us (2%)
    pallas_call x1, Pallas kernels, local(): pl.pallas_call(functools.partial(fine_kernel, sources), in_specs=[pl.Bloc...  8.99 us
    ppermute x4, starting transfers between devices, crossed(): lax.ppermute(array, 'trial', [(place, place ^ step) for place in range(so...  5.02 us
    ppermute x3, starting transfers between devices, sent(): lax.ppermute(sums, 'band', [(place, partner(place, step)) for place in ra...  4.8 us
    ppermute x4, waiting for transfers between devices, crossed(): lax.ppermute(array, 'trial', [(place, place ^ step) for place in range(so...  4.45 us
    ppermute x3, waiting for transfers between devices, sent(): lax.ppermute(sums, 'band', [(place, partner(place, step)) for place in ra...  3.45 us
    pallas_call x2, Pallas kernels, more(): pl.pallas_call(functools.partial(next_kernel, subs, beams, some, count),...  3.27 us
    pallas_call x1, Pallas kernels, local(): pl.pallas_call(functools.partial(peak_kernel, beams, math.sqrt(channels *...  1.67 us
    pallas_call x1, Pallas kernels, local(): pl.pallas_call(functools.partial(first_kernel, subs, beams, packed, steps...  1.33 us
  transfers between devices with their start and end apart: 7, of which 6 were waited for; matrix products, arithmetic and copies ran while one was open for 2% of the time, Pallas kernels for 9%

profile of v6, /device:TPU:0, one launch (start us, length us, event | category | flops | bytes accessed | tf_op | source)
XLA Modules:
  0.0 34.5 jit_solution(5955134288988805275)
XLA Ops:
  0.6 9.0 %fine_delays.1 = (bf16[4,144,128]{2,1,0:T(8,128)(2,1)S(1)}, bf16[4,144,128]{2,1,0:T(8,128)(2,1)S(1)}) custom-call(s32[8,32]{1,0:T(8,128)} %span_any.1, bf16[2,4096,256]{2,1,0:T(8,128)(2,1)} %x_hbm.1, s32[8,32,512]{2,1,0:T(8,128)} %delay_hbm.1), custom_call_target="tpu_custom_call" | custom-call | tf_op jit(solution)/shard_map/fine_delays/pallas_call | solution.py:315
  9.6 0.5 %collective-permute-start = (bf16[4,144,128]{2,1,0:T(8,128)(2,1)S(1)}, bf16[4,144,128]{2,1,0:T(8,128)(2,1)S(1)}, u32[]{:S(2)}, u32[]{:S(2)}) collective-permute-start(bf16[4,144,128]{2,1,0:T(8,128)(2,1)S(1)} %get-tuple-element.15), channel_id=1, source_target_pairs={{0,1},{1,0},{2,3},{3,2},{4,5},{5,4},{6,7},{7,6},{8,9},{9,8},{10,11... | collective-permute-start | bytes 442376 | tf_op jit(solution)/shard_map/ppermute | solution.py:340
  10.1 1.0 %collective-permute-done.swap_ref = bf16[4,144,128]{2,1,0:T(8,128)(2,1)S(1)} collective-permute-done((bf16[4,144,128]{2,1,0:T(8,128)(2,1)S(1)}, bf16[4,144,128]{2,1,0:T(8,128)(2,1)S(1)}, u32[]{:S(2)}, u32[]{:S(2)}) %collective-permute-start) | collective-permute-done | bytes 147488 | tf_op jit(solution)/shard_map/ppermute | solution.py:340
  11.2 3.9 %collective-permute-start.1 = (bf16[2,144,128]{2,1,0:T(8,128)(2,1)S(1)}, bf16[2,144,128]{2,1,0:T(8,128)(2,1)S(1)}, u32[]{:S(2)}, u32[]{:S(2)}) collective-permute-start(bf16[2,144,128]{2,1,0:T(8,128)(2,1)S(1)} %get-tuple-element.16), channel_id=1, source_target_pairs={{0,6},{1,7},{2,4},{3,5},{4,2},{5,3},{6,0},{7,1},{8,14},{9,15},{10,... | collective-permute-start | bytes 221192 | tf_op jit(solution)/shard_map/ppermute | solution.py:340
  15.0 0.5 %collective-permute-start.2 = (bf16[2,144,128]{2,1,0:T(8,128)(2,1)S(1)}, bf16[2,144,128]{2,1,0:T(8,128)(2,1)S(1)}, u32[]{:S(2)}, u32[]{:S(2)}) collective-permute-start(bf16[2,144,128]{2,1,0:T(8,128)(2,1)S(1)} %get-tuple-element.17), channel_id=1, source_target_pairs={{0,4},{1,5},{2,6},{3,7},{4,0},{5,1},{6,2},{7,3},{8,12},{9,13},{10,... | collective-permute-start | bytes 221192 | tf_op jit(solution)/shard_map/ppermute | solution.py:340
  15.5 0.1 collective-permute-start.3
  15.7 0.8 %add_bitcast_fusion.place_any.place_ref = s32[8,64]{1,0:T(8,128)S(1)} fusion(s32[64,32]{0,1:T(8,128)} %param.10, s32[]{:T(128)S(6)} %select_n.4, s32[64,32]{0,1:T(8,128)} %param.9, s32[8]{0:T(128)S(1)} %iota_multiply_fusion), kind=kLoop, calls=%fused_computation.1 | loop fusion | flops 1536 | bytes 6180 | tf_op jit(solution)/shard_map/add | solution.py:337
  16.5 1.2 %collective-permute-done.1.refs_0_ = bf16[2,144,128]{2,1,0:T(8,128)(2,1)S(1)} collective-permute-done((bf16[2,144,128]{2,1,0:T(8,128)(2,1)S(1)}, bf16[2,144,128]{2,1,0:T(8,128)(2,1)S(1)}, u32[]{:S(2)}, u32[]{:S(2)}) %collective-permute-start.1) | collective-permute-done | bytes 73760 | tf_op jit(solution)/shard_map/ppermute | solution.py:340
  17.7 1.7 %collective-permute-done.2.refs_1_ = bf16[2,144,128]{2,1,0:T(8,128)(2,1)S(1)} collective-permute-done((bf16[2,144,128]{2,1,0:T(8,128)(2,1)S(1)}, bf16[2,144,128]{2,1,0:T(8,128)(2,1)S(1)}, u32[]{:S(2)}, u32[]{:S(2)}) %collective-permute-start.2) | collective-permute-done | bytes 73760 | tf_op jit(solution)/shard_map/ppermute | solution.py:340
  19.4 0.5 %collective-permute-done.3.refs_2_ = bf16[2,144,128]{2,1,0:T(8,128)(2,1)S(1)} collective-permute-done((bf16[2,144,128]{2,1,0:T(8,128)(2,1)S(1)}, bf16[2,144,128]{2,1,0:T(8,128)(2,1)S(1)}, u32[]{:S(2)}, u32[]{:S(2)}) %collective-permute-start.3) | collective-permute-done | bytes 73760 | tf_op jit(solution)/shard_map/ppermute | solution.py:340
  19.9 1.3 %spread_and_add.1 = (f32[64,32,128]{2,1,0:T(8,128)S(1)}, bf16[16,32,128]{2,1,0:T(8,128)(2,1)S(1)}) custom-call(s32[8,64]{1,0:T(8,128)S(1)} %add_bitcast_fusion.place_any.place_ref, bf16[2,144,128]{2,1,0:T(8,128)(2,1)S(1)} %collective-permute-done.1.refs_0_, bf16[2,144,128]{2,1,0:T(8,128)(2,1)S(1)} %collective-permute-done.2.refs_1_, ...), custom_call_target="tpu_custom_call" | custom-call | tf_op jit(solution)/shard_map/spread_and_add/pallas_call | solution.py:356
  21.2 1.7 %collective-permute-start.4 = (bf16[16,32,128]{2,1,0:T(8,128)(2,1)S(1)}, bf16[16,32,128]{2,1,0:T(8,128)(2,1)S(1)}, u32[]{:S(2)}, u32[]{:S(2)}) collective-permute-start(bf16[16,32,128]{2,1,0:T(8,128)(2,1)S(1)} %get-tuple-element.22), channel_id=1, source_target_pairs={{0,8},{8,0},{16,24},{24,16},{1,9},{9,1},{17,25},{25,17},{2,10},{10... | collective-permute-start | bytes 393224 | tf_op jit(solution)/shard_map/ppermute | solution.py:383
  22.9 1.9 %add_trials.3 = (f32[16,32,128]{2,1,0:T(8,128)S(1)}, bf16[16,32,128]{2,1,0:T(8,128)(2,1)S(1)}) custom-call(s32[8,64]{1,0:T(8,128)S(1)} %add_bitcast_fusion.place_any.place_ref, f32[64,32,128]{2,1,0:T(8,128)S(1)} %get-tuple-element.20.wide_ref), custom_call_target="tpu_custom_call" | custom-call | flops 2147483648 | bytes 8388608 | tf_op jit(solution)/shard_map/add_trials/pallas_call | solution.py:371
  24.8 0.0 copy-start
  24.9 0.5 %collective-permute-start.6 = (bf16[16,32,128]{2,1,0:T(8,128)(2,1)S(1)}, bf16[16,32,128]{2,1,0:T(8,128)(2,1)S(1)}, u32[]{:S(2)}, u32[]{:S(2)}) collective-permute-start(bf16[16,32,128]{2,1,0:T(8,128)(2,1)S(1)} %get-tuple-element.23), channel_id=1, source_target_pairs={{0,8},{8,0},{16,24},{24,16},{1,9},{9,1},{17,25},{25,17},{2,10},{10... | collective-permute-start | bytes 393224 | tf_op jit(solution)/shard_map/ppermute | solution.py:383
  25.4 1.3 %collective-permute-done.4 = bf16[16,32,128]{2,1,0:T(8,128)(2,1)S(1)} collective-permute-done((bf16[16,32,128]{2,1,0:T(8,128)(2,1)S(1)}, bf16[16,32,128]{2,1,0:T(8,128)(2,1)S(1)}, u32[]{:S(2)}, u32[]{:S(2)}) %collective-permute-start.4) | collective-permute-done | bytes 131104 | tf_op jit(solution)/shard_map/ppermute | solution.py:383
  26.7 2.6 %collective-permute-start.5 = (bf16[16,32,128]{2,1,0:T(8,128)(2,1)S(1)}, bf16[16,32,128]{2,1,0:T(8,128)(2,1)S(1)}, u32[]{:S(2)}, u32[]{:S(2)}) collective-permute-start(bf16[16,32,128]{2,1,0:T(8,128)(2,1)S(1)} %add_convert_fusion), channel_id=1, source_target_pairs={{0,16},{8,24},{16,0},{24,8},{1,17},{9,25},{17,1},{25,9},{2,18},{10... | collective-permute-start | bytes 393224 | tf_op jit(solution)/shard_map/ppermute | solution.py:383
  29.3 1.3 %add_trials.2.refs_0_ = f32[16,32,128]{2,1,0:T(8,128)S(1)} custom-call(s32[8,64]{1,0:T(8,128)S(1)} %add_bitcast_fusion.place_any.place_ref, f32[64,32,128]{2,1,0:T(8,128)S(1)} %get-tuple-element.20.wide_ref), custom_call_target="tpu_custom_call" | custom-call | flops 1073741824 | bytes 4194304 | tf_op jit(solution)/shard_map/add_trials/pallas_call | solution.py:371
  30.7 0.0 collective-permute-done.6.refs_2_
  30.7 2.2 %collective-permute-done.5.refs_1_ = bf16[16,32,128]{2,1,0:T(8,128)(2,1)S(1)} collective-permute-done((bf16[16,32,128]{2,1,0:T(8,128)(2,1)S(1)}, bf16[16,32,128]{2,1,0:T(8,128)(2,1)S(1)}, u32[]{:S(2)}, u32[]{:S(2)}) %collective-permute-start.5) | collective-permute-done | bytes 131104 | tf_op jit(solution)/shard_map/ppermute | solution.py:383
  32.8 0.0 copy-done
  32.8 1.7 %boxcar_peaks.1 = (bf16[2,16,2048]{2,1,0:T(8,128)(2,1)}, f32[2,4,16]{2,1,0:T(4,128)}) custom-call(s32[4]{0:T(128)S(1)} %copy-done, f32[16,32,128]{2,1,0:T(8,128)S(1)} %add_trials.2.refs_0_, bf16[16,32,128]{2,1,0:T(8,128)(2,1)S(1)} %collective-permute-done.5.refs_1_, bf16[16,32,128]{2,1,0:T(8,128)(2,1)S(1)} %collective-permute-done.6.refs_2_), custom_call_target="tpu_custom_call" | custom-call | tf_op jit(solution)/shard_map/boxcar_peaks/pallas_call | solution.py:391
  (3 shorter events, 0.1 us)
Async XLA Ops:
  9.6 1.5 %collective-permute-start = (bf16[4,144,128]{2,1,0:T(8,128)(2,1)S(1)}, bf16[4,144,128]{2,1,0:T(8,128)(2,1)S(1)}, u32[]{:S(2)}, u32[]{:S(2)}) collective-permute-start(bf16[4,144,128]{2,1,0:T(8,128)(2,1)S(1)} %get-tuple-element.15), channel_id=1, source_target_pairs={{0,1},{1,0},{2,3},{3,2},{4,5},{5,4},{6,7},{7,6},{8,9},{9,8},{10,11... | collective-permute-start | bytes 442376 | tf_op jit(solution)/shard_map/ppermute | solution.py:340
  11.2 6.5 %collective-permute-start.1 = (bf16[2,144,128]{2,1,0:T(8,128)(2,1)S(1)}, bf16[2,144,128]{2,1,0:T(8,128)(2,1)S(1)}, u32[]{:S(2)}, u32[]{:S(2)}) collective-permute-start(bf16[2,144,128]{2,1,0:T(8,128)(2,1)S(1)} %get-tuple-element.16), channel_id=1, source_target_pairs={{0,6},{1,7},{2,4},{3,5},{4,2},{5,3},{6,0},{7,1},{8,14},{9,15},{10,... | collective-permute-start | bytes 221192 | tf_op jit(solution)/shard_map/ppermute | solution.py:340
  15.0 4.4 %collective-permute-start.2 = (bf16[2,144,128]{2,1,0:T(8,128)(2,1)S(1)}, bf16[2,144,128]{2,1,0:T(8,128)(2,1)S(1)}, u32[]{:S(2)}, u32[]{:S(2)}) collective-permute-start(bf16[2,144,128]{2,1,0:T(8,128)(2,1)S(1)} %get-tuple-element.17), channel_id=1, source_target_pairs={{0,4},{1,5},{2,6},{3,7},{4,0},{5,1},{6,2},{7,3},{8,12},{9,13},{10,... | collective-permute-start | bytes 221192 | tf_op jit(solution)/shard_map/ppermute | solution.py:340
  15.5 4.4 %collective-permute-start.3 = (bf16[2,144,128]{2,1,0:T(8,128)(2,1)S(1)}, bf16[2,144,128]{2,1,0:T(8,128)(2,1)S(1)}, u32[]{:S(2)}, u32[]{:S(2)}) collective-permute-start(bf16[2,144,128]{2,1,0:T(8,128)(2,1)S(1)} %get-tuple-element.18), channel_id=1, source_target_pairs={{0,2},{1,3},{2,0},{3,1},{4,6},{5,7},{6,4},{7,5},{8,10},{9,11},{10,... | collective-permute-start | bytes 221192 | tf_op jit(solution)/shard_map/ppermute | solution.py:340
  21.2 5.4 %collective-permute-start.4 = (bf16[16,32,128]{2,1,0:T(8,128)(2,1)S(1)}, bf16[16,32,128]{2,1,0:T(8,128)(2,1)S(1)}, u32[]{:S(2)}, u32[]{:S(2)}) collective-permute-start(bf16[16,32,128]{2,1,0:T(8,128)(2,1)S(1)} %get-tuple-element.22), channel_id=1, source_target_pairs={{0,8},{8,0},{16,24},{24,16},{1,9},{9,1},{17,25},{25,17},{2,10},{10... | collective-permute-start | bytes 393224 | tf_op jit(solution)/shard_map/ppermute | solution.py:383
  24.8 8.0 %copy-start = (s32[4]{0:T(128)S(1)}, s32[4]{0:T(128)}, u32[]{:S(2)}) copy-start(s32[4]{0:T(128)} %width_any.1) | copy-start | bytes 52
  24.9 5.8 %collective-permute-start.6 = (bf16[16,32,128]{2,1,0:T(8,128)(2,1)S(1)}, bf16[16,32,128]{2,1,0:T(8,128)(2,1)S(1)}, u32[]{:S(2)}, u32[]{:S(2)}) collective-permute-start(bf16[16,32,128]{2,1,0:T(8,128)(2,1)S(1)} %get-tuple-element.23), channel_id=1, source_target_pairs={{0,8},{8,0},{16,24},{24,16},{1,9},{9,1},{17,25},{25,17},{2,10},{10... | collective-permute-start | bytes 393224 | tf_op jit(solution)/shard_map/ppermute | solution.py:383
  26.7 6.2 %collective-permute-start.5 = (bf16[16,32,128]{2,1,0:T(8,128)(2,1)S(1)}, bf16[16,32,128]{2,1,0:T(8,128)(2,1)S(1)}, u32[]{:S(2)}, u32[]{:S(2)}) collective-permute-start(bf16[16,32,128]{2,1,0:T(8,128)(2,1)S(1)} %add_convert_fusion), channel_id=1, source_target_pairs={{0,16},{8,24},{16,0},{24,8},{1,17},{9,25},{17,1},{25,9},{2,18},{10... | collective-permute-start | bytes 393224 | tf_op jit(solution)/shard_map/ppermute | solution.py:383

commit v7 on v6

--- a/solution.py
+++ b/solution.py
@@ -262,7 +262,8 @@
         total = x_refs[0][block].astype(jnp.float32)
         for x_ref in x_refs[1:]:
             total = total + x_ref[block].astype(jnp.float32)
-        series.append((total / scale).astype(jnp.bfloat16))
+        total = total * (1 / scale) if math.frexp(scale)[0] == 0.5 else total / scale
+        series.append(total.astype(jnp.bfloat16))
     for block in range(blocks):
         for beam in range(beams):
             series_ref[beam, :, block * LANES : (block + 1) * LANES] = (

time: 35.2 us -> 35.2 us (level)
  no operation moved by 1% of the time
where the time goes in v7:
time: 35.2 us; the launch traced here: 34.5 us
  Pallas kernels  15.3 us (43%)
  starting transfers between devices  9.82 us (28%)
  waiting for transfers between devices  7.89 us (22%)
  other arithmetic  0.81 us (2%)
  between operations  0.69 us (2%)
    pallas_call x1, Pallas kernels, local(): pl.pallas_call(functools.partial(fine_kernel, sources), in_specs=[pl.Bloc...  8.99 us
    ppermute x4, starting transfers between devices, crossed(): lax.ppermute(array, 'trial', [(place, place ^ step) for place in range(so...  5.02 us
    ppermute x3, starting transfers between devices, sent(): lax.ppermute(sums, 'band', [(place, partner(place, step)) for place in ra...  4.8 us
    ppermute x4, waiting for transfers between devices, crossed(): lax.ppermute(array, 'trial', [(place, place ^ step) for place in range(so...  4.45 us
    ppermute x3, waiting for transfers between devices, sent(): lax.ppermute(sums, 'band', [(place, partner(place, step)) for place in ra...  3.45 us
    pallas_call x2, Pallas kernels, more(): pl.pallas_call(functools.partial(next_kernel, subs, beams, some, count),...  3.27 us
    pallas_call x1, Pallas kernels, local(): pl.pallas_call(functools.partial(peak_kernel, beams, math.sqrt(channels *...  1.68 us
    pallas_call x1, Pallas kernels, local(): pl.pallas_call(functools.partial(first_kernel, subs, beams, packed, steps...  1.33 us
  transfers between devices with their start and end apart: 7, of which 6 were waited for; matrix products, arithmetic and copies ran while one was open for 2% of the time, Pallas kernels for 9%

profile of v7, /device:TPU:0, one launch (start us, length us, event | category | flops | bytes accessed | tf_op | source)
XLA Modules:
  0.0 34.5 jit_solution(5955134288988805275)
XLA Ops:
  0.6 9.0 %fine_delays.1 = (bf16[4,144,128]{2,1,0:T(8,128)(2,1)S(1)}, bf16[4,144,128]{2,1,0:T(8,128)(2,1)S(1)}) custom-call(s32[8,32]{1,0:T(8,128)} %span_any.1, bf16[2,4096,256]{2,1,0:T(8,128)(2,1)} %x_hbm.1, s32[8,32,512]{2,1,0:T(8,128)} %delay_hbm.1), custom_call_target="tpu_custom_call" | custom-call | tf_op jit(solution)/shard_map/fine_delays/pallas_call | solution.py:316
  9.6 0.5 %collective-permute-start = (bf16[4,144,128]{2,1,0:T(8,128)(2,1)S(1)}, bf16[4,144,128]{2,1,0:T(8,128)(2,1)S(1)}, u32[]{:S(2)}, u32[]{:S(2)}) collective-permute-start(bf16[4,144,128]{2,1,0:T(8,128)(2,1)S(1)} %get-tuple-element.15), channel_id=1, source_target_pairs={{0,1},{1,0},{2,3},{3,2},{4,5},{5,4},{6,7},{7,6},{8,9},{9,8},{10,11... | collective-permute-start | bytes 442376 | tf_op jit(solution)/shard_map/ppermute | solution.py:341
  10.1 1.0 %collective-permute-done.swap_ref = bf16[4,144,128]{2,1,0:T(8,128)(2,1)S(1)} collective-permute-done((bf16[4,144,128]{2,1,0:T(8,128)(2,1)S(1)}, bf16[4,144,128]{2,1,0:T(8,128)(2,1)S(1)}, u32[]{:S(2)}, u32[]{:S(2)}) %collective-permute-start) | collective-permute-done | bytes 147488 | tf_op jit(solution)/shard_map/ppermute | solution.py:341
  11.2 3.9 %collective-permute-start.1 = (bf16[2,144,128]{2,1,0:T(8,128)(2,1)S(1)}, bf16[2,144,128]{2,1,0:T(8,128)(2,1)S(1)}, u32[]{:S(2)}, u32[]{:S(2)}) collective-permute-start(bf16[2,144,128]{2,1,0:T(8,128)(2,1)S(1)} %get-tuple-element.16), channel_id=1, source_target_pairs={{0,6},{1,7},{2,4},{3,5},{4,2},{5,3},{6,0},{7,1},{8,14},{9,15},{10,... | collective-permute-start | bytes 221192 | tf_op jit(solution)/shard_map/ppermute | solution.py:341
  15.0 0.5 %collective-permute-start.2 = (bf16[2,144,128]{2,1,0:T(8,128)(2,1)S(1)}, bf16[2,144,128]{2,1,0:T(8,128)(2,1)S(1)}, u32[]{:S(2)}, u32[]{:S(2)}) collective-permute-start(bf16[2,144,128]{2,1,0:T(8,128)(2,1)S(1)} %get-tuple-element.17), channel_id=1, source_target_pairs={{0,4},{1,5},{2,6},{3,7},{4,0},{5,1},{6,2},{7,3},{8,12},{9,13},{10,... | collective-permute-start | bytes 221192 | tf_op jit(solution)/shard_map/ppermute | solution.py:341
  15.5 0.1 collective-permute-start.3
  15.7 0.8 %add_bitcast_fusion.place_any.place_ref = s32[8,64]{1,0:T(8,128)S(1)} fusion(s32[64,32]{0,1:T(8,128)} %param.10, s32[]{:T(128)S(6)} %select_n.4, s32[64,32]{0,1:T(8,128)} %param.9, s32[8]{0:T(128)S(1)} %iota_multiply_fusion), kind=kLoop, calls=%fused_computation.1 | loop fusion | flops 1536 | bytes 6180 | tf_op jit(solution)/shard_map/add | solution.py:338
  16.5 1.2 %collective-permute-done.1.refs_0_ = bf16[2,144,128]{2,1,0:T(8,128)(2,1)S(1)} collective-permute-done((bf16[2,144,128]{2,1,0:T(8,128)(2,1)S(1)}, bf16[2,144,128]{2,1,0:T(8,128)(2,1)S(1)}, u32[]{:S(2)}, u32[]{:S(2)}) %collective-permute-start.1) | collective-permute-done | bytes 73760 | tf_op jit(solution)/shard_map/ppermute | solution.py:341
  17.7 1.7 %collective-permute-done.2.refs_1_ = bf16[2,144,128]{2,1,0:T(8,128)(2,1)S(1)} collective-permute-done((bf16[2,144,128]{2,1,0:T(8,128)(2,1)S(1)}, bf16[2,144,128]{2,1,0:T(8,128)(2,1)S(1)}, u32[]{:S(2)}, u32[]{:S(2)}) %collective-permute-start.2) | collective-permute-done | bytes 73760 | tf_op jit(solution)/shard_map/ppermute | solution.py:341
  19.4 0.5 %collective-permute-done.3.refs_2_ = bf16[2,144,128]{2,1,0:T(8,128)(2,1)S(1)} collective-permute-done((bf16[2,144,128]{2,1,0:T(8,128)(2,1)S(1)}, bf16[2,144,128]{2,1,0:T(8,128)(2,1)S(1)}, u32[]{:S(2)}, u32[]{:S(2)}) %collective-permute-start.3) | collective-permute-done | bytes 73760 | tf_op jit(solution)/shard_map/ppermute | solution.py:341
  19.9 1.3 %spread_and_add.1 = (f32[64,32,128]{2,1,0:T(8,128)S(1)}, bf16[16,32,128]{2,1,0:T(8,128)(2,1)S(1)}) custom-call(s32[8,64]{1,0:T(8,128)S(1)} %add_bitcast_fusion.place_any.place_ref, bf16[2,144,128]{2,1,0:T(8,128)(2,1)S(1)} %collective-permute-done.1.refs_0_, bf16[2,144,128]{2,1,0:T(8,128)(2,1)S(1)} %collective-permute-done.2.refs_1_, ...), custom_call_target="tpu_custom_call" | custom-call | tf_op jit(solution)/shard_map/spread_and_add/pallas_call | solution.py:357
  21.2 1.7 %collective-permute-start.4 = (bf16[16,32,128]{2,1,0:T(8,128)(2,1)S(1)}, bf16[16,32,128]{2,1,0:T(8,128)(2,1)S(1)}, u32[]{:S(2)}, u32[]{:S(2)}) collective-permute-start(bf16[16,32,128]{2,1,0:T(8,128)(2,1)S(1)} %get-tuple-element.22), channel_id=1, source_target_pairs={{0,8},{8,0},{16,24},{24,16},{1,9},{9,1},{17,25},{25,17},{2,10},{10... | collective-permute-start | bytes 393224 | tf_op jit(solution)/shard_map/ppermute | solution.py:384
  22.9 1.9 %add_trials.3 = (f32[16,32,128]{2,1,0:T(8,128)S(1)}, bf16[16,32,128]{2,1,0:T(8,128)(2,1)S(1)}) custom-call(s32[8,64]{1,0:T(8,128)S(1)} %add_bitcast_fusion.place_any.place_ref, f32[64,32,128]{2,1,0:T(8,128)S(1)} %get-tuple-element.20.wide_ref), custom_call_target="tpu_custom_call" | custom-call | flops 2147483648 | bytes 8388608 | tf_op jit(solution)/shard_map/add_trials/pallas_call | solution.py:372
  24.8 0.0 copy-start
  24.9 0.5 %collective-permute-start.6 = (bf16[16,32,128]{2,1,0:T(8,128)(2,1)S(1)}, bf16[16,32,128]{2,1,0:T(8,128)(2,1)S(1)}, u32[]{:S(2)}, u32[]{:S(2)}) collective-permute-start(bf16[16,32,128]{2,1,0:T(8,128)(2,1)S(1)} %get-tuple-element.23), channel_id=1, source_target_pairs={{0,8},{8,0},{16,24},{24,16},{1,9},{9,1},{17,25},{25,17},{2,10},{10... | collective-permute-start | bytes 393224 | tf_op jit(solution)/shard_map/ppermute | solution.py:384
  25.4 1.3 %collective-permute-done.4 = bf16[16,32,128]{2,1,0:T(8,128)(2,1)S(1)} collective-permute-done((bf16[16,32,128]{2,1,0:T(8,128)(2,1)S(1)}, bf16[16,32,128]{2,1,0:T(8,128)(2,1)S(1)}, u32[]{:S(2)}, u32[]{:S(2)}) %collective-permute-start.4) | collective-permute-done | bytes 131104 | tf_op jit(solution)/shard_map/ppermute | solution.py:384
  26.7 2.6 %collective-permute-start.5 = (bf16[16,32,128]{2,1,0:T(8,128)(2,1)S(1)}, bf16[16,32,128]{2,1,0:T(8,128)(2,1)S(1)}, u32[]{:S(2)}, u32[]{:S(2)}) collective-permute-start(bf16[16,32,128]{2,1,0:T(8,128)(2,1)S(1)} %add_convert_fusion), channel_id=1, source_target_pairs={{0,16},{8,24},{16,0},{24,8},{1,17},{9,25},{17,1},{25,9},{2,18},{10... | collective-permute-start | bytes 393224 | tf_op jit(solution)/shard_map/ppermute | solution.py:384
  29.3 1.3 %add_trials.2.refs_0_ = f32[16,32,128]{2,1,0:T(8,128)S(1)} custom-call(s32[8,64]{1,0:T(8,128)S(1)} %add_bitcast_fusion.place_any.place_ref, f32[64,32,128]{2,1,0:T(8,128)S(1)} %get-tuple-element.20.wide_ref), custom_call_target="tpu_custom_call" | custom-call | flops 1073741824 | bytes 4194304 | tf_op jit(solution)/shard_map/add_trials/pallas_call | solution.py:372
  30.7 0.0 collective-permute-done.6.refs_2_
  30.7 2.2 %collective-permute-done.5.refs_1_ = bf16[16,32,128]{2,1,0:T(8,128)(2,1)S(1)} collective-permute-done((bf16[16,32,128]{2,1,0:T(8,128)(2,1)S(1)}, bf16[16,32,128]{2,1,0:T(8,128)(2,1)S(1)}, u32[]{:S(2)}, u32[]{:S(2)}) %collective-permute-start.5) | collective-permute-done | bytes 131104 | tf_op jit(solution)/shard_map/ppermute | solution.py:384
  32.8 0.0 copy-done
  32.8 1.7 %boxcar_peaks.1 = (bf16[2,16,2048]{2,1,0:T(8,128)(2,1)}, f32[2,4,16]{2,1,0:T(4,128)}) custom-call(s32[4]{0:T(128)S(1)} %copy-done, f32[16,32,128]{2,1,0:T(8,128)S(1)} %add_trials.2.refs_0_, bf16[16,32,128]{2,1,0:T(8,128)(2,1)S(1)} %collective-permute-done.5.refs_1_, bf16[16,32,128]{2,1,0:T(8,128)(2,1)S(1)} %collective-permute-done.6.refs_2_), custom_call_target="tpu_custom_call" | custom-call | tf_op jit(solution)/shard_map/boxcar_peaks/pallas_call | solution.py:392
  (3 shorter events, 0.1 us)
Async XLA Ops:
  9.6 1.5 %collective-permute-start = (bf16[4,144,128]{2,1,0:T(8,128)(2,1)S(1)}, bf16[4,144,128]{2,1,0:T(8,128)(2,1)S(1)}, u32[]{:S(2)}, u32[]{:S(2)}) collective-permute-start(bf16[4,144,128]{2,1,0:T(8,128)(2,1)S(1)} %get-tuple-element.15), channel_id=1, source_target_pairs={{0,1},{1,0},{2,3},{3,2},{4,5},{5,4},{6,7},{7,6},{8,9},{9,8},{10,11... | collective-permute-start | bytes 442376 | tf_op jit(solution)/shard_map/ppermute | solution.py:341
  11.2 6.5 %collective-permute-start.1 = (bf16[2,144,128]{2,1,0:T(8,128)(2,1)S(1)}, bf16[2,144,128]{2,1,0:T(8,128)(2,1)S(1)}, u32[]{:S(2)}, u32[]{:S(2)}) collective-permute-start(bf16[2,144,128]{2,1,0:T(8,128)(2,1)S(1)} %get-tuple-element.16), channel_id=1, source_target_pairs={{0,6},{1,7},{2,4},{3,5},{4,2},{5,3},{6,0},{7,1},{8,14},{9,15},{10,... | collective-permute-start | bytes 221192 | tf_op jit(solution)/shard_map/ppermute | solution.py:341
  15.0 4.4 %collective-permute-start.2 = (bf16[2,144,128]{2,1,0:T(8,128)(2,1)S(1)}, bf16[2,144,128]{2,1,0:T(8,128)(2,1)S(1)}, u32[]{:S(2)}, u32[]{:S(2)}) collective-permute-start(bf16[2,144,128]{2,1,0:T(8,128)(2,1)S(1)} %get-tuple-element.17), channel_id=1, source_target_pairs={{0,4},{1,5},{2,6},{3,7},{4,0},{5,1},{6,2},{7,3},{8,12},{9,13},{10,... | collective-permute-start | bytes 221192 | tf_op jit(solution)/shard_map/ppermute | solution.py:341
  15.5 4.4 %collective-permute-start.3 = (bf16[2,144,128]{2,1,0:T(8,128)(2,1)S(1)}, bf16[2,144,128]{2,1,0:T(8,128)(2,1)S(1)}, u32[]{:S(2)}, u32[]{:S(2)}) collective-permute-start(bf16[2,144,128]{2,1,0:T(8,128)(2,1)S(1)} %get-tuple-element.18), channel_id=1, source_target_pairs={{0,2},{1,3},{2,0},{3,1},{4,6},{5,7},{6,4},{7,5},{8,10},{9,11},{10,... | collective-permute-start | bytes 221192 | tf_op jit(solution)/shard_map/ppermute | solution.py:341
  21.2 5.4 %collective-permute-start.4 = (bf16[16,32,128]{2,1,0:T(8,128)(2,1)S(1)}, bf16[16,32,128]{2,1,0:T(8,128)(2,1)S(1)}, u32[]{:S(2)}, u32[]{:S(2)}) collective-permute-start(bf16[16,32,128]{2,1,0:T(8,128)(2,1)S(1)} %get-tuple-element.22), channel_id=1, source_target_pairs={{0,8},{8,0},{16,24},{24,16},{1,9},{9,1},{17,25},{25,17},{2,10},{10... | collective-permute-start | bytes 393224 | tf_op jit(solution)/shard_map/ppermute | solution.py:384
  24.8 8.0 %copy-start = (s32[4]{0:T(128)S(1)}, s32[4]{0:T(128)}, u32[]{:S(2)}) copy-start(s32[4]{0:T(128)} %width_any.1) | copy-start | bytes 52
  24.9 5.8 %collective-permute-start.6 = (bf16[16,32,128]{2,1,0:T(8,128)(2,1)S(1)}, bf16[16,32,128]{2,1,0:T(8,128)(2,1)S(1)}, u32[]{:S(2)}, u32[]{:S(2)}) collective-permute-start(bf16[16,32,128]{2,1,0:T(8,128)(2,1)S(1)} %get-tuple-element.23), channel_id=1, source_target_pairs={{0,8},{8,0},{16,24},{24,16},{1,9},{9,1},{17,25},{25,17},{2,10},{10... | collective-permute-start | bytes 393224 | tf_op jit(solution)/shard_map/ppermute | solution.py:384
  26.7 6.2 %collective-permute-start.5 = (bf16[16,32,128]{2,1,0:T(8,128)(2,1)S(1)}, bf16[16,32,128]{2,1,0:T(8,128)(2,1)S(1)}, u32[]{:S(2)}, u32[]{:S(2)}) collective-permute-start(bf16[16,32,128]{2,1,0:T(8,128)(2,1)S(1)} %add_convert_fusion), channel_id=1, source_target_pairs={{0,16},{8,24},{16,0},{24,8},{1,17},{9,25},{17,1},{25,9},{2,18},{10... | collective-permute-start | bytes 393224 | tf_op jit(solution)/shard_map/ppermute | solution.py:384
